TPU v7x, 32 devices: a whole 2x2x4 slice. The times are simulated.
32 devices in a mesh: groups: 2 (over x), tile: 16 (over z, y, core).
Axes of the slice: x: 2, y: 2, z: 4, core: 2. Of those that a mesh axis runs over, the one named last changes fastest.
Arguments:
- tiles: float32 [2, 12288, 384], P(None, ('groups', 'tile')), parts along dimension 1, may hold values from -6 to 6
- library: float32 [128, 2, 128, 128], P('tile'), may hold values from -6 to 6
- block_owner: int32 [2], replicated, may hold values from 0 to 15
- block_clips: int32 [2, 2], replicated, may hold values from 0 to 7
- layer_order: int32 [32, 2], P(('groups', 'tile')), parts along dimension 0, may hold values from 0 to 1, each once within a row
Outputs:
- scores: float32 [2, 2, 12288, 384], P(None, None, ('groups', 'tile')), parts along dimension 2
- peak_scores: float32 [4, 2], P('groups'), parts along dimension 0
There are 2 independent parts, one for each index of `groups`. A program takes and returns all parts, laid end to end along the dimension named above; an argument that names none is the same for every part. Nothing has to cross between parts.
Inputs may be any that keep to these rules, and one draw needn't show every extreme that they name: `layer_order`: each row is a permutation of 0 to 1.
All inputs are finite; a program needn't handle non-finite values.
Results may differ from a plain program's by a relative error of at most 0.000098.
Values sent between devices are 32-bit elements; how exact they have to be, the bound alone decides.
No kernel may reach another device: no remote copies, remote signals or barrier semaphores. Data moves between devices by JAX's collectives and lax.ppermute only.
A program may use at most 128 MiB of HBM per device.

v0:
```python
import math

import jax
import jax.numpy as jnp
import ml_dtypes
import numpy as np
from jax import lax
from jax.experimental import pallas as pl
from jax.experimental.pallas import tpu as pltpu
from jax.sharding import PartitionSpec as P

SIGNS = (math.sqrt(2.0), -math.sqrt(2.0))


def halves(matrix):
    high = matrix.astype(ml_dtypes.bfloat16)
    low = (matrix - high.astype(np.float64)).astype(ml_dtypes.bfloat16)
    return high, low


def evaluation(e, ring):
    k = np.arange(2 * e)
    k = k[np.isin(k % 4, (0, 3) if ring == 0 else (1, 2))]
    angles = np.outer(2 * k + 1, np.arange(2 * e)) % (8 * e) * (2.0 * np.pi / (8 * e))
    return np.concatenate([np.cos(angles), np.sin(angles)], axis=0)


def left_factor(matrix):
    high, low = halves(matrix)
    return np.concatenate([high, low, high], axis=1)


def right_factor(matrix):
    high, low = halves(matrix)
    return np.concatenate([high, low, high], axis=0)


def factors(e):
    ev = [evaluation(e, ring) for ring in range(2)]
    inv = [np.linalg.inv(m) / (4.0 * math.sqrt(2.0)) for m in ev]
    inv_cols = [np.linalg.inv(m) / (2.0 * math.sqrt(2.0)) for m in ev]
    tile_left = np.stack([left_factor(m) for m in ev])
    tile_right = np.stack([right_factor(m.T) for m in ev])
    clip_left = left_factor(np.concatenate([m[:, :e] for m in ev], axis=0))
    clip_right = right_factor(np.concatenate([m[:, :e].T for m in ev], axis=1))
    back_left = np.stack([left_factor(m) for m in inv])
    back_right = np.stack([right_factor(m.T) for m in inv_cols])
    return tile_left, tile_right, clip_left, clip_right, back_left, back_right


def bands(e):
    position = np.arange(2 * e)[None, :] - np.arange(e)[:, None]
    band = ((position >= 0) & (position < e)).astype(ml_dtypes.bfloat16)
    return np.concatenate([band, band], axis=1), np.concatenate([band.T, band.T], axis=0)


def split(values):
    high = values.astype(jnp.bfloat16)
    return high, (values - high.astype(jnp.float32)).astype(jnp.bfloat16)


def dot(a, b):
    return jnp.dot(a, b, preferred_element_type=jnp.float32)


def beside(values):
    high, low = split(values)
    return jnp.concatenate([high, high, low], axis=1)


def stacked(values):
    high, low = split(values)
    return jnp.concatenate([high, high, low], axis=0)


def tile_kernel(tile, halo, left, right, band_rows, band_cols, spectrum, inverse_rms):
    layers, rows, columns = tile.shape
    e = halo.shape[1]
    blocks = [[tile[l, b * e : (b + 1) * e, :] for b in range(3)] + [halo[l]] for l in range(layers)]
    for l in range(layers):
        a0, a1, a2, a3 = blocks[l]
        for si, s in enumerate(SIGNS):
            folded = jnp.concatenate([a0 - a2 - s * a3, a1 + s * a2 + a3], axis=0)
            c0, c1, c2 = (folded[:, b * e : (b + 1) * e] for b in range(3))
            along = []
            for ti, t in enumerate(SIGNS):
                ring = jnp.concatenate([c0 - c2, c1 + t * c2], axis=1)
                along.append(dot(beside(ring), right[ti]))
            both = dot(left[si], stacked(jnp.concatenate(along, axis=1)))
            for ti in range(2):
                at = ti * 2 * e
                cc, cs = both[:e, at : at + e], both[:e, at + e : at + 2 * e]
                sc, ss = both[e:, at : at + e], both[e:, at + e : at + 2 * e]
                lanes = slice(ti * e, (ti + 1) * e)
                place = slice(si * e, (si + 1) * e)
                spectrum[l, 0, place, lanes] = cc - ss
                spectrum[l, 1, place, lanes] = -(cs + sc)
                spectrum[l, 2, place, lanes] = cc + ss
                spectrum[l, 3, place, lanes] = sc - cs
    squares = [sum(blocks[l][b] * blocks[l][b] for l in range(layers)) for b in range(4)]
    parts = [split(v) for v in squares]
    for b in range(3):
        tall = jnp.concatenate([parts[b][0], parts[b + 1][0], parts[b][1], parts[b + 1][1]], axis=0)
        summed = dot(band_rows[...], tall)
        high, low = split(summed)
        for c in range(3):
            pair = (high[:, c * e : (c + 2) * e], low[:, c * e : (c + 2) * e])
            if c < 2:
                energy = dot(jnp.concatenate(pair, axis=1), band_cols[...])
            else:
                energy = dot(pair[0], band_cols[:e, :]) + dot(pair[1], band_cols[:e, :])
            inverse_rms[b * e : (b + 1) * e, c * e : (c + 1) * e] = lax.rsqrt(
                energy * (1.0 / (layers * e * e)) + 1e-05
            )


def score_kernel(
    slots, order, clip, spectrum, inverse_rms, clip_left, clip_right, back_left, back_right, *rest
):
    scores, peaks = rest[-2:]
    layers, e, _ = clip.shape
    root = math.sqrt(layers * e * e)
    first = [clip[order[l]] for l in range(layers)]
    total = sum(jnp.sum(v * v, keepdims=True) for v in first)
    scale = lax.rsqrt(total * (1.0 / (layers * e * e)) + 1e-05) * (1.0 / root)
    along = dot(beside(jnp.concatenate(first, axis=0)), clip_right[...])
    both = [dot(clip_left[...], stacked(along[l * e : (l + 1) * e])) for l in range(layers)]
    rows = []
    for si in range(2):
        upper, lower = [], []
        for ti in range(2):
            at, up = ti * 2 * e, si * 2 * e
            rp = ip = rm = im = 0.0
            for l in range(layers):
                cc, cs = both[l][up : up + e, at : at + e], both[l][up : up + e, at + e : at + 2 * e]
                sc = both[l][up + e : up + 2 * e, at : at + e]
                ss = both[l][up + e : up + 2 * e, at + e : at + 2 * e]
                xpr, xpi, xmr, xmi = (
                    spectrum[l, j, si * e : (si + 1) * e, ti * e : (ti + 1) * e] for j in range(4)
                )
                kpr, kpi, kmr, kmi = cc - ss, cs + sc, cc + ss, sc - cs
                rp = rp + (xpr * kpr - xpi * kpi)
                ip = ip + (xpi * kpr + xpr * kpi)
                rm = rm + (xmr * kmr + xmi * kmi)
                im = im + (xmi * kmr - xmr * kmi)
            upper += [rp + rm, -(ip + im)]
            lower += [im - ip, rm - rp]
        rows.append(
            jnp.concatenate([jnp.concatenate(upper, axis=1), jnp.concatenate(lower, axis=1)], axis=0)
        )
    p, m = (dot(back_left[si], stacked(rows[si])) for si in range(2))
    b2 = p[e:] - m[e:]
    b0 = SIGNS[0] * (p[:e] + m[:e]) + b2
    b1 = SIGNS[0] * (p[e:] + m[e:]) + (p[:e] - m[:e])
    back = jnp.concatenate([b0, b1, b2], axis=0)
    p, m = (
        dot(beside(back[:, ti * 2 * e : (ti + 1) * 2 * e]), back_right[ti]) for ti in range(2)
    )
    b2 = p[:, e:] - m[:, e:]
    b0 = SIGNS[0] * (p[:, :e] + m[:, :e]) + b2
    b1 = SIGNS[0] * (p[:, e:] + m[:, e:]) + (p[:, :e] - m[:, :e])
    result = jnp.concatenate([b0, b1, b2], axis=1) * inverse_rms[...] * scale
    scores[...] = result
    largest = jnp.max(result)
    i = pl.program_id(0)

    @pl.when(i == 0)
    def _():
        peaks[...] = jnp.full(peaks.shape, -jnp.inf, jnp.float32)

    row = lax.broadcasted_iota(jnp.int32, peaks.shape, 0)
    peaks[...] = jnp.where(row == slots[i], largest, peaks[...])


def whole(array):
    return pl.BlockSpec(array.shape, lambda *_: (0,) * array.ndim)


def tile_call(tiles, halo, consts):
    layers, rows, columns = tiles.shape
    e = halo.shape[1]
    args = (tiles, halo) + consts
    return pl.pallas_call(
        tile_kernel,
        out_shape=(
            jax.ShapeDtypeStruct((layers, 4, 2 * e, 2 * e), jnp.float32),
            jax.ShapeDtypeStruct((rows, columns), jnp.float32),
        ),
        compiler_params=pltpu.CompilerParams(vmem_limit_bytes=48 * 1024 * 1024),
        cost_estimate=pl.CostEstimate(flops=2_000_000_000, bytes_accessed=6_000_000, transcendentals=0),
    )(*args)


def score_call(slots, order, clips, spectrum, inverse_rms, consts, count, before):
    n, layers, e, _ = clips.shape
    rows, columns = inverse_rms.shape
    fixed = (spectrum, inverse_rms) + consts
    in_specs = [pl.BlockSpec((None, layers, e, e), lambda i, *_: (i, 0, 0, 0))]
    in_specs += [whole(a) for a in fixed]
    args = (clips,) + fixed
    aliases = {}
    if before is not None:
        in_specs.append(pl.BlockSpec(memory_space=pl.ANY))
        args += (before,)
        aliases = {2 + len(args) - 1: 0}
    return pl.pallas_call(
        score_kernel,
        grid_spec=pltpu.PrefetchScalarGridSpec(
            num_scalar_prefetch=2,
            grid=(n,),
            in_specs=in_specs,
            out_specs=(
                pl.BlockSpec((None, rows, columns), lambda i, slots, order: (slots[i], 0, 0)),
                pl.BlockSpec((8, 128), lambda i, *_: (0, 0)),
            ),
        ),
        out_shape=(
            jax.ShapeDtypeStruct((count, rows, columns), jnp.float32),
            jax.ShapeDtypeStruct((8, 128), jnp.float32),
        ),
        input_output_aliases=aliases,
        compiler_params=pltpu.CompilerParams(
            vmem_limit_bytes=56 * 1024 * 1024, dimension_semantics=("arbitrary",)
        ),
        cost_estimate=pl.CostEstimate(
            flops=n * 1_300_000_000, bytes_accessed=6_000_000, transcendentals=0
        ),
    )(slots, order, *args)


def swap(block, axis, distance):
    return lax.ppermute(block, axis, [(i, i ^ distance) for i in range(lax.axis_size(axis))])


def local(tiles, library, block_owner, block_clips, layer_order):
    layers, rows, columns = tiles.shape
    e = library.shape[-1]
    assert rows == 3 * e and columns == 3 * e and layers * e <= 256
    blocks, per_block = block_clips.shape
    devices = lax.axis_size("tile")
    assert blocks == 2 and per_block == 2 and devices & (devices - 1) == 0
    tile_left, tile_right, clip_left, clip_right, back_left, back_right = map(jnp.asarray, factors(e))
    band_rows, band_cols = map(jnp.asarray, bands(e))

    me = lax.axis_index("tile")
    core = me % 2
    block = lax.axis_index("groups") % 2
    owner = block_owner[block]
    chosen = lax.dynamic_index_in_dim(block_clips, block, 0, keepdims=False)
    mine = lax.dynamic_index_in_dim(library, chosen[core], 0, keepdims=False)
    theirs = lax.dynamic_index_in_dim(library, chosen[1 - core], 0, keepdims=False)
    differ = owner ^ me
    got = swap(theirs, "tile", 1)
    held = jnp.where((differ & 1) == 0, mine, got)
    distance = 2
    while distance < devices:
        got = swap(held, "tile", distance)
        held = jnp.where((differ & distance) == 0, held, got)
        distance *= 2
    other = swap(held, "groups", 1)
    rest = swap(jnp.stack([held, other]), "tile", 1)
    later = jnp.concatenate([other[None], rest], axis=0)

    route = [(i, i - 1) for i in range(1, devices)]
    halo = lax.ppermute(tiles[:, :e, :], "tile", route)
    spectrum, inverse_rms = tile_call(
        tiles, halo, (tile_left, tile_right, band_rows, band_cols)
    )
    consts = (clip_left, clip_right, back_left, back_right)
    order = layer_order[0]
    count = blocks * per_block
    slot = block * per_block + core
    first = slot[None].astype(jnp.int32)
    second = jnp.stack([slot ^ 2, slot ^ 1, slot ^ 3]).astype(jnp.int32)
    scores, peaks = score_call(first, order, held[None], spectrum, inverse_rms, consts, count, None)
    scores, more = score_call(second, order, later, spectrum, inverse_rms, consts, count, scores)
    best = jnp.maximum(peaks, more)
    distance = 1
    while distance < devices:
        best = jnp.maximum(best, swap(best, "tile", distance))
        distance *= 2
    return (
        scores.reshape(blocks, per_block, rows, columns),
        best[:count, 0].reshape(blocks, per_block),
    )


def solution(mesh):
    in_specs = (
        P(None, ("groups", "tile"), None),
        P("tile", None, None, None),
        P(),
        P(),
        P(("groups", "tile"), None),
    )
    out_specs = (P(None, None, ("groups", "tile"), None), P("groups", None))
    return jax.shard_map(local, mesh=mesh, in_specs=in_specs, out_specs=out_specs, check_vma=False)
```

profile of v0, /device:TPU:0, one launch (start us, length us, event | category | flops | bytes accessed | tf_op | source)
XLA Modules:
  0.0 76.8 jit_solution(199026774042807742)
XLA Ops:
  0.6 0.0 copy-start.5
  0.6 0.0 copy-start.6
  0.7 0.0 copy-start.3
  0.7 0.0 copy-start.4
  0.7 0.0 copy-start.2
  0.7 1.4 %fusion = (s32[1,1]{1,0:T(1,128)}, s32[1,1]{1,0:T(1,128)}) fusion(s32[2,2]{1,0:T(2,128)} %param.16, s32[]{:T(128)S(6)} %select_n.68, s32[]{:T(128)S(6)} %select_n.70, s32[]{:T(128)S(6)} %select_n.73), kind=kLoop, calls=%fused_computation.9 | loop fusion | bytes 28 | tf_op jit(solution)/shard_map/dynamic_slice | solution.py:250
  4.1 0.9 %dynamic-slice_bitcast_fusion = f32[2,128,128]{2,1,0:T(8,128)S(1)} fusion(f32[8,2,128,128]{3,2,1,0:T(8,128)} %param.14, s32[]{:T(128)S(6)} %select_n.74), kind=kLoop, calls=%fused_computation.3 | loop fusion | bytes 262148 | tf_op jit(solution)/shard_map/jit(dynamic_index_in_dim)/squeeze | solution.py:251
  5.0 0.5 collective-permute-start
  6.9 1.2 %dynamic_slice.18 = s32[1]{0:T(128)} dynamic-slice(s32[2]{0:T(128)} %param.15, s32[]{:T(128)S(6)} %select_n.63), dynamic_slice_sizes={1} | dynamic-slice | bytes 12 | tf_op jit(solution)/shard_map/dynamic_slice | solution.py:248
  9.4 0.0 collective-permute-done
  9.4 0.9 %bitcast_select_fusion = f32[2,128,128]{2,1,0:T(8,128)S(1)} fusion(f32[2,128,128]{2,1,0:T(8,128)S(1)} %collective-permute-done, f32[8,2,128,128]{3,2,1,0:T(8,128)} %param.14, s32[]{:T(128)S(6)} %select_n.71, pred[]{:T(512)S(6)} %eq.18), kind=kLoop, calls=%fused_computation.2 | loop fusion | flops 32768 | bytes 393221 | tf_op jit(solution)/shard_map/jit(_where)/select_n | solution.py:254
  10.3 2.6 %collective-permute-start.1 = (f32[2,128,128]{2,1,0:T(8,128)S(1)}, f32[2,128,128]{2,1,0:T(8,128)S(1)}, u32[]{:S(2)}, u32[]{:S(2)}) collective-permute-start(f32[2,128,128]{2,1,0:T(8,128)S(1)} %bitcast_select_fusion), channel_id=1, source_target_pairs={{0,2},{1,3},{2,0},{3,1},{4,6},{5,7},{6,4},{7,5},{8,10},{9,11},{10,... | collective-permute-start | bytes 393224 | tf_op jit(solution)/shard_map/ppermute | solution.py:232
  12.9 4.2 %collective-permute-done.1 = f32[2,128,128]{2,1,0:T(8,128)S(1)} collective-permute-done((f32[2,128,128]{2,1,0:T(8,128)S(1)}, f32[2,128,128]{2,1,0:T(8,128)S(1)}, u32[]{:S(2)}, u32[]{:S(2)}) %collective-permute-start.1) | collective-permute-done | bytes 131104 | tf_op jit(solution)/shard_map/ppermute | solution.py:232
  17.1 1.9 %collective-permute-start.2 = (f32[2,128,128]{2,1,0:T(8,128)S(1)}, f32[2,128,128]{2,1,0:T(8,128)S(1)}, u32[]{:S(2)}, u32[]{:S(2)}) collective-permute-start(f32[2,128,128]{2,1,0:T(8,128)S(1)} %broadcast_select_fusion), channel_id=1, source_target_pairs={{0,4},{1,5},{2,6},{3,7},{4,0},{5,1},{6,2},{7,3},{8,12},{9,13},{10,... | collective-permute-start | bytes 393224 | tf_op jit(solution)/shard_map/ppermute | solution.py:232
  19.0 3.5 %collective-permute-done.2 = f32[2,128,128]{2,1,0:T(8,128)S(1)} collective-permute-done((f32[2,128,128]{2,1,0:T(8,128)S(1)}, f32[2,128,128]{2,1,0:T(8,128)S(1)}, u32[]{:S(2)}, u32[]{:S(2)}) %collective-permute-start.2) | collective-permute-done | bytes 131104 | tf_op jit(solution)/shard_map/ppermute | solution.py:232
  22.5 0.0 copy-start.8
  22.5 2.7 %collective-permute-start.3 = (f32[2,128,128]{2,1,0:T(8,128)S(1)}, f32[2,128,128]{2,1,0:T(8,128)}, u32[]{:S(2)}, u32[]{:S(2)}) collective-permute-start(f32[2,128,128]{2,1,0:T(8,128)S(1)} %broadcast_select_fusion.1), channel_id=1, source_target_pairs={{0,8},{1,9},{2,10},{3,11},{4,12},{5,13},{6,14},{7,15},{8,0},{9,1},... | collective-permute-start | bytes 393224 | tf_op jit(solution)/shard_map/ppermute | solution.py:232
  25.2 1.8 %slice.6 = f32[2,128,384]{2,1,0:T(8,128)} slice(f32[2,384,384]{2,1,0:T(8,128)} %tile.1), slice={[0:2], [0:128], [0:384]} | slice | bytes 786432 | tf_op jit(solution)/shard_map/slice | solution.py:265
  27.0 1.3 %collective-permute-start.6 = (f32[2,128,384]{2,1,0:T(8,128)}, f32[2,128,384]{2,1,0:T(8,128)S(1)}, u32[]{:S(2)}, u32[]{:S(2)}) collective-permute-start(f32[2,128,384]{2,1,0:T(8,128)} %slice.6), channel_id=1, source_target_pairs={{1,0},{2,1},{3,2},{4,3},{5,4},{6,5},{7,6},{8,7},{9,8},{10,9},{11,1... | collective-permute-start | bytes 1179656 | tf_op jit(solution)/shard_map/ppermute | solution.py:265
  28.3 0.0 copy-done.8
  28.3 2.6 %collective-permute-done.3 = f32[2,128,128]{2,1,0:T(8,128)} collective-permute-done((f32[2,128,128]{2,1,0:T(8,128)S(1)}, f32[2,128,128]{2,1,0:T(8,128)}, u32[]{:S(2)}, u32[]{:S(2)}) %collective-permute-start.3) | collective-permute-done | bytes 131104 | tf_op jit(solution)/shard_map/ppermute | solution.py:232
  30.9 0.9 %broadcast_select_fusion.2 = f32[2,128,128]{2,1,0:T(8,128)S(1)} fusion(f32[2,128,128]{2,1,0:T(8,128)} %copy-done.8, f32[2,128,128]{2,1,0:T(8,128)} %collective-permute-done.3, pred[]{:T(512)S(6)} %eq.15), kind=kLoop, calls=%fused_computation.6 | loop fusion | flops 32768 | bytes 393217 | tf_op jit(solution)/shard_map/jit(_where)/select_n | solution.py:258
  31.8 0.0 copy-start.7
  31.8 1.3 %collective-permute-start.4 = (f32[2,128,128]{2,1,0:T(8,128)S(1)}, f32[2,128,128]{2,1,0:T(8,128)}, u32[]{:S(2)}, u32[]{:S(2)}) collective-permute-start(f32[2,128,128]{2,1,0:T(8,128)S(1)} %broadcast_select_fusion.2), channel_id=1, source_target_pairs={{0,16},{16,0},{1,17},{17,1},{2,18},{18,2},{3,19},{19,3},{4,20},{20... | collective-permute-start | bytes 393224 | tf_op jit(solution)/shard_map/ppermute | solution.py:232
  33.2 0.6 pad_add_fusion.slots
  33.8 3.2 %collective-permute-done.4 = f32[2,128,128]{2,1,0:T(8,128)} collective-permute-done((f32[2,128,128]{2,1,0:T(8,128)S(1)}, f32[2,128,128]{2,1,0:T(8,128)}, u32[]{:S(2)}, u32[]{:S(2)}) %collective-permute-start.4) | collective-permute-done | bytes 131104 | tf_op jit(solution)/shard_map/ppermute | solution.py:232
  36.9 0.9 %pad_maximum_fusion.1 = f32[2,2,128,128]{3,2,1,0:T(8,128)S(1)} fusion(f32[1,2,128,128]{3,2,1,0:T(8,128)} %bitcast.9, f32[1,2,128,128]{3,2,1,0:T(8,128)S(1)} %bitcast.15), kind=kLoop, calls=%fused_computation.1 | loop fusion | flops 65536 | bytes 524288 | tf_op jit(solution)/shard_map/stack | solution.py:261
  37.9 0.1 collective-permute-start.5
  38.0 0.0 collective-permute-done.6.halo
  38.0 0.0 copy-done.5
  38.0 0.0 copy-done.6
  38.0 0.0 copy-done.3
  38.0 0.0 copy-done.4
  38.0 0.0 copy-done.2
  38.0 3.2 %shard_map.140 = (f32[2,4,256,256]{3,2,1,0:T(8,128)S(1)}, f32[384,384]{1,0:T(8,128)S(1)}) custom-call(f32[2,384,384]{2,1,0:T(8,128)S(1)} %copy-done.2, f32[2,128,384]{2,1,0:T(8,128)S(1)} %collective-permute-done.6.halo, bf16[2,256,768]{2,1,0:T(8,128)(2,1)S(1)} %copy-done.4, bf16[2,768,256]{2,1,0:T(8,128)(2,1)S(1)} %copy-done.3, ...), custom_call_target="tpu_custom_call" | custom-call | flops 2000000000 | bytes 6000000 | tf_op jit(solution)/shard_map/pallas_call | solution.py:183
  41.2 0.0 copy-done.7
  41.2 0.0 copy-start
  41.2 1.3 %copy-done = f32[2,4,256,256]{3,2,1,0:T(8,128)} copy-done((f32[2,4,256,256]{3,2,1,0:T(8,128)}, f32[2,4,256,256]{3,2,1,0:T(8,128)S(1)}, u32[]{:S(2)}) %copy-start) | copy-done | bytes 2097176
  42.5 0.0 copy-start.1
  42.5 0.8 %copy-done.1 = f32[384,384]{1,0:T(8,128)} copy-done((f32[384,384]{1,0:T(8,128)}, f32[384,384]{1,0:T(8,128)S(1)}, u32[]{:S(2)}) %copy-start.1) | copy-done | bytes 589848
  43.3 6.1 %shard_map.141 = (f32[4,384,384]{2,1,0:T(8,128)}, f32[8,128]{1,0:T(8,128)}) custom-call(s32[1]{0:T(128)} %bitcast.11.slots, s32[2]{0:T(128)} %bitcast.17, f32[1,2,128,128]{3,2,1,0:T(8,128)} %bitcast.16, f32[2,4,256,256]{3,2,1,0:T(8,128)} %copy-done, f32[384,384]{1,0:T(8,128)} %copy-done.1, bf16[512,384]{1,0:T(8,128)(2,1)} %constant.85.clone.clip_left, ...), custom_call_target="tpu_custom_call" | custom-call | flops 1300000000 | bytes 6000000 | tf_op jit(solution)/shard_map/pallas_call | solution.py:206
  49.5 0.0 collective-permute-done.5
  49.5 1.7 %pad_maximum_fusion.clip = f32[3,2,128,128]{3,2,1,0:T(8,128)} fusion(f32[2,2,128,128]{3,2,1,0:T(8,128)S(1)} %collective-permute-done.5, f32[1,2,128,128]{3,2,1,0:T(8,128)} %bitcast.9), kind=kLoop, calls=%fused_computation | loop fusion | flops 98304 | bytes 786432 | tf_op jit(solution)/shard_map/concatenate | solution.py:262
  51.2 0.0 copy-start.9
  51.2 11.2 %shard_map.142 = (f32[4,384,384]{2,1,0:T(8,128)}, f32[8,128]{1,0:T(8,128)}) custom-call(s32[3]{0:T(128)} %pad_add_fusion.slots, s32[2]{0:T(128)} %bitcast.18, f32[3,2,128,128]{3,2,1,0:T(8,128)} %pad_maximum_fusion.clip, f32[2,4,256,256]{3,2,1,0:T(8,128)} %copy-done, f32[384,384]{1,0:T(8,128)} %copy-done.1, ...), custom_call_target="tpu_custom_call", output_to_operand_aliasing={{0}: (9, {})} | custom-call | flops 3900000000 | bytes 6000000 | tf_op jit(solution)/shard_map/pallas_call | solution.py:206
  62.3 0.0 copy-done.9
  62.3 0.7 max.15
  63.0 0.5 collective-permute-start.7
  63.5 0.8 %collective-permute-done.7 = f32[8,128]{1,0:T(8,128)S(1)} collective-permute-done((f32[8,128]{1,0:T(8,128)S(1)}, f32[8,128]{1,0:T(8,128)S(1)}, u32[]{:S(2)}, u32[]{:S(2)}) %collective-permute-start.7) | collective-permute-done | bytes 4128 | tf_op jit(solution)/shard_map/ppermute | solution.py:232
  64.3 1.3 %collective-permute-start.8 = (f32[8,128]{1,0:T(8,128)S(1)}, f32[8,128]{1,0:T(8,128)S(1)}, u32[]{:S(2)}, u32[]{:S(2)}) collective-permute-start(f32[8,128]{1,0:T(8,128)S(1)} %max.16), channel_id=1, source_target_pairs={{0,2},{1,3},{2,0},{3,1},{4,6},{5,7},{6,4},{7,5},{8,10},{9,11},{10,... | collective-permute-start | bytes 12296 | tf_op jit(solution)/shard_map/ppermute | solution.py:232
  65.6 2.3 %collective-permute-done.8 = f32[8,128]{1,0:T(8,128)S(1)} collective-permute-done((f32[8,128]{1,0:T(8,128)S(1)}, f32[8,128]{1,0:T(8,128)S(1)}, u32[]{:S(2)}, u32[]{:S(2)}) %collective-permute-start.8) | collective-permute-done | bytes 4128 | tf_op jit(solution)/shard_map/ppermute | solution.py:232
  67.9 0.6 collective-permute-start.9
  68.5 3.1 %collective-permute-done.9 = f32[8,128]{1,0:T(8,128)S(1)} collective-permute-done((f32[8,128]{1,0:T(8,128)S(1)}, f32[8,128]{1,0:T(8,128)S(1)}, u32[]{:S(2)}, u32[]{:S(2)}) %collective-permute-start.9) | collective-permute-done | bytes 4128 | tf_op jit(solution)/shard_map/ppermute | solution.py:232
  71.6 1.8 %collective-permute-start.10 = (f32[8,128]{1,0:T(8,128)S(1)}, f32[8,128]{1,0:T(8,128)S(1)}, u32[]{:S(2)}, u32[]{:S(2)}) collective-permute-start(f32[8,128]{1,0:T(8,128)S(1)} %max.18), channel_id=1, source_target_pairs={{0,8},{1,9},{2,10},{3,11},{4,12},{5,13},{6,14},{7,15},{8,0},{9,1},... | collective-permute-start | bytes 12296 | tf_op jit(solution)/shard_map/ppermute | solution.py:232
  73.4 2.7 %collective-permute-done.10 = f32[8,128]{1,0:T(8,128)S(1)} collective-permute-done((f32[8,128]{1,0:T(8,128)S(1)}, f32[8,128]{1,0:T(8,128)S(1)}, u32[]{:S(2)}, u32[]{:S(2)}) %collective-permute-start.10) | collective-permute-done | bytes 4128 | tf_op jit(solution)/shard_map/ppermute | solution.py:232
  76.1 0.1 slice_reduce_fusion
  76.2 0.6 reshape_squeeze.3
  (6 shorter events, 0.0 us)
Async XLA Ops:
  0.6 37.3 %copy-start.5 = (bf16[512,128]{1,0:T(8,128)(2,1)S(1)}, bf16[512,128]{1,0:T(8,128)(2,1)}, u32[]{:S(2)}) copy-start(bf16[512,128]{1,0:T(8,128)(2,1)} %constant.90.clone.band_cols) | copy-start | bytes 393220
  0.6 37.3 %copy-start.6 = (bf16[128,512]{1,0:T(8,128)(2,1)S(1)}, bf16[128,512]{1,0:T(8,128)(2,1)}, u32[]{:S(2)}) copy-start(bf16[128,512]{1,0:T(8,128)(2,1)} %constant.89.clone.band_rows) | copy-start | bytes 393220
  0.7 37.3 %copy-start.3 = (bf16[2,768,256]{2,1,0:T(8,128)(2,1)S(1)}, bf16[2,768,256]{2,1,0:T(8,128)(2,1)}, u32[]{:S(2)}) copy-start(bf16[2,768,256]{2,1,0:T(8,128)(2,1)} %constant.84.clone.right) | copy-start | bytes 2359300
  0.7 37.3 %copy-start.4 = (bf16[2,256,768]{2,1,0:T(8,128)(2,1)S(1)}, bf16[2,256,768]{2,1,0:T(8,128)(2,1)}, u32[]{:S(2)}) copy-start(bf16[2,256,768]{2,1,0:T(8,128)(2,1)} %constant.83.clone.left) | copy-start | bytes 2359300
  0.7 37.3 %copy-start.2 = (f32[2,384,384]{2,1,0:T(8,128)S(1)}, f32[2,384,384]{2,1,0:T(8,128)}, u32[]{:S(2)}) copy-start(f32[2,384,384]{2,1,0:T(8,128)} %tile.1) | copy-start | bytes 3538948
  5.0 4.4 %collective-permute-start = (f32[2,128,128]{2,1,0:T(8,128)S(1)}, f32[2,128,128]{2,1,0:T(8,128)S(1)}, u32[]{:S(2)}, u32[]{:S(2)}) collective-permute-start(f32[2,128,128]{2,1,0:T(8,128)S(1)} %dynamic-slice_bitcast_fusion), channel_id=1, source_target_pairs={{0,1},{1,0},{2,3},{3,2},{4,5},{5,4},{6,7},{7,6},{8,9},{9,8},{10,11... | collective-permute-start | bytes 393224 | tf_op jit(solution)/shard_map/ppermute | solution.py:232
  10.3 6.8 %collective-permute-start.1 = (f32[2,128,128]{2,1,0:T(8,128)S(1)}, f32[2,128,128]{2,1,0:T(8,128)S(1)}, u32[]{:S(2)}, u32[]{:S(2)}) collective-permute-start(f32[2,128,128]{2,1,0:T(8,128)S(1)} %bitcast_select_fusion), channel_id=1, source_target_pairs={{0,2},{1,3},{2,0},{3,1},{4,6},{5,7},{6,4},{7,5},{8,10},{9,11},{10,... | collective-permute-start | bytes 393224 | tf_op jit(solution)/shard_map/ppermute | solution.py:232
  17.1 5.4 %collective-permute-start.2 = (f32[2,128,128]{2,1,0:T(8,128)S(1)}, f32[2,128,128]{2,1,0:T(8,128)S(1)}, u32[]{:S(2)}, u32[]{:S(2)}) collective-permute-start(f32[2,128,128]{2,1,0:T(8,128)S(1)} %broadcast_select_fusion), channel_id=1, source_target_pairs={{0,4},{1,5},{2,6},{3,7},{4,0},{5,1},{6,2},{7,3},{8,12},{9,13},{10,... | collective-permute-start | bytes 393224 | tf_op jit(solution)/shard_map/ppermute | solution.py:232
  22.5 5.7 %copy-start.8 = (f32[2,128,128]{2,1,0:T(8,128)}, f32[2,128,128]{2,1,0:T(8,128)S(1)}, u32[]{:S(2)}) copy-start(f32[2,128,128]{2,1,0:T(8,128)S(1)} %broadcast_select_fusion.1) | copy-start | bytes 393220
  22.5 8.3 %collective-permute-start.3 = (f32[2,128,128]{2,1,0:T(8,128)S(1)}, f32[2,128,128]{2,1,0:T(8,128)}, u32[]{:S(2)}, u32[]{:S(2)}) collective-permute-start(f32[2,128,128]{2,1,0:T(8,128)S(1)} %broadcast_select_fusion.1), channel_id=1, source_target_pairs={{0,8},{1,9},{2,10},{3,11},{4,12},{5,13},{6,14},{7,15},{8,0},{9,1},... | collective-permute-start | bytes 393224 | tf_op jit(solution)/shard_map/ppermute | solution.py:232
  27.0 11.0 %collective-permute-start.6 = (f32[2,128,384]{2,1,0:T(8,128)}, f32[2,128,384]{2,1,0:T(8,128)S(1)}, u32[]{:S(2)}, u32[]{:S(2)}) collective-permute-start(f32[2,128,384]{2,1,0:T(8,128)} %slice.6), channel_id=1, source_target_pairs={{1,0},{2,1},{3,2},{4,3},{5,4},{6,5},{7,6},{8,7},{9,8},{10,9},{11,1... | collective-permute-start | bytes 1179656 | tf_op jit(solution)/shard_map/ppermute | solution.py:265
  31.8 9.4 %copy-start.7 = (f32[2,128,128]{2,1,0:T(8,128)}, f32[2,128,128]{2,1,0:T(8,128)S(1)}, u32[]{:S(2)}) copy-start(f32[2,128,128]{2,1,0:T(8,128)S(1)} %broadcast_select_fusion.2) | copy-start | bytes 393220
  31.8 5.1 %collective-permute-start.4 = (f32[2,128,128]{2,1,0:T(8,128)S(1)}, f32[2,128,128]{2,1,0:T(8,128)}, u32[]{:S(2)}, u32[]{:S(2)}) collective-permute-start(f32[2,128,128]{2,1,0:T(8,128)S(1)} %broadcast_select_fusion.2), channel_id=1, source_target_pairs={{0,16},{16,0},{1,17},{17,1},{2,18},{18,2},{3,19},{19,3},{4,20},{20... | collective-permute-start | bytes 393224 | tf_op jit(solution)/shard_map/ppermute | solution.py:232
  37.9 11.6 %collective-permute-start.5 = (f32[2,2,128,128]{3,2,1,0:T(8,128)S(1)}, f32[2,2,128,128]{3,2,1,0:T(8,128)S(1)}, u32[]{:S(2)}, u32[]{:S(2)}) collective-permute-start(f32[2,2,128,128]{3,2,1,0:T(8,128)S(1)} %pad_maximum_fusion.1), channel_id=1, source_target_pairs={{0,1},{1,0},{2,3},{3,2},{4,5},{5,4},{6,7},{7,6},{8,9},{9,8},{10,11... | collective-permute-start | bytes 786440 | tf_op jit(solution)/shard_map/ppermute | solution.py:232
  41.2 1.3 %copy-start = (f32[2,4,256,256]{3,2,1,0:T(8,128)}, f32[2,4,256,256]{3,2,1,0:T(8,128)S(1)}, u32[]{:S(2)}) copy-start(f32[2,4,256,256]{3,2,1,0:T(8,128)S(1)} %get-tuple-element.8.spectrum) | copy-start | bytes 6291460
  42.5 0.8 %copy-start.1 = (f32[384,384]{1,0:T(8,128)}, f32[384,384]{1,0:T(8,128)S(1)}, u32[]{:S(2)}) copy-start(f32[384,384]{1,0:T(8,128)S(1)} %get-tuple-element.9.inverse_rms) | copy-start | bytes 1769476
  51.2 11.2 %copy-start.9 = (f32[8,128]{1,0:T(8,128)S(1)}, f32[8,128]{1,0:T(8,128)}, u32[]{:S(2)}) copy-start(f32[8,128]{1,0:T(8,128)} %get-tuple-element.12) | copy-start | bytes 12292
  63.0 1.3 %collective-permute-start.7 = (f32[8,128]{1,0:T(8,128)S(1)}, f32[8,128]{1,0:T(8,128)S(1)}, u32[]{:S(2)}, u32[]{:S(2)}) collective-permute-start(f32[8,128]{1,0:T(8,128)S(1)} %max.15), channel_id=1, source_target_pairs={{0,1},{1,0},{2,3},{3,2},{4,5},{5,4},{6,7},{7,6},{8,9},{9,8},{10,11... | collective-permute-start | bytes 12296 | tf_op jit(solution)/shard_map/ppermute | solution.py:232
  64.3 3.6 %collective-permute-start.8 = (f32[8,128]{1,0:T(8,128)S(1)}, f32[8,128]{1,0:T(8,128)S(1)}, u32[]{:S(2)}, u32[]{:S(2)}) collective-permute-start(f32[8,128]{1,0:T(8,128)S(1)} %max.16), channel_id=1, source_target_pairs={{0,2},{1,3},{2,0},{3,1},{4,6},{5,7},{6,4},{7,5},{8,10},{9,11},{10,... | collective-permute-start | bytes 12296 | tf_op jit(solution)/shard_map/ppermute | solution.py:232
  67.9 3.6 %collective-permute-start.9 = (f32[8,128]{1,0:T(8,128)S(1)}, f32[8,128]{1,0:T(8,128)S(1)}, u32[]{:S(2)}, u32[]{:S(2)}) collective-permute-start(f32[8,128]{1,0:T(8,128)S(1)} %max.17), channel_id=1, source_target_pairs={{0,4},{1,5},{2,6},{3,7},{4,0},{5,1},{6,2},{7,3},{8,12},{9,13},{10,... | collective-permute-start | bytes 12296 | tf_op jit(solution)/shard_map/ppermute | solution.py:232
  71.6 4.5 %collective-permute-start.10 = (f32[8,128]{1,0:T(8,128)S(1)}, f32[8,128]{1,0:T(8,128)S(1)}, u32[]{:S(2)}, u32[]{:S(2)}) collective-permute-start(f32[8,128]{1,0:T(8,128)S(1)} %max.18), channel_id=1, source_target_pairs={{0,8},{1,9},{2,10},{3,11},{4,12},{5,13},{6,14},{7,15},{8,0},{9,1},... | collective-permute-start | bytes 12296 | tf_op jit(solution)/shard_map/ppermute | solution.py:232
where the time goes:
time: 77.3 us; the launch traced here: 76.8 us
  waiting for transfers between devices  22.4 us (29%)
  Pallas kernels  20.5 us (27%)
  starting transfers between devices  14.5 us (19%)
  local copies, waits for them, and re-layouts  8.33 us (11%)
  other arithmetic  5.78 us (7%)
  between operations  5.42 us (7%)
    ppermute x10, waiting for transfers between devices, swap(): lax.ppermute(block, axis, [(i, i ^ distance) for i in range(lax.axis_size...  22.4 us
    pallas_call x2, Pallas kernels, score_call(): pl.pallas_call(score_kernel, grid_spec=pltpu.PrefetchScalarGridSpec(num_s...  17.3 us
    ppermute x10, starting transfers between devices, swap(): lax.ppermute(block, axis, [(i, i ^ distance) for i in range(lax.axis_size...  13.2 us
    pallas_call x1, Pallas kernels, tile_call(): pl.pallas_call(tile_kernel, out_shape=(jax.ShapeDtypeStruct((layers, 4, 2...  3.16 us
    unnamed x20, local copies, waits for them, and re-layouts  2.19 us
    slice x1, local copies, waits for them, and re-layouts, local(): halo = lax.ppermute(tiles[:, :e, :], 'tile', route)  1.77 us
    concatenate x1, other arithmetic, local(): later = jnp.concatenate([other[None], rest], axis=0)  1.69 us
  transfers between devices with their start and end apart: 11, of which 8 were waited for; matrix products, arithmetic and copies ran while one was open for 7% of the time, Pallas kernels for 12%

commit v1 on v0

--- a/solution.py
+++ b/solution.py
@@ -10,6 +10,9 @@
 from jax.sharding import PartitionSpec as P
 
 SIGNS = (math.sqrt(2.0), -math.sqrt(2.0))
+VMEM = 20 * 1024 * 1024
+MOST = 40 * 1024 * 1024
+WHOLE = 57 * 1024 * 1024
 
 
 def halves(matrix):
@@ -73,10 +76,25 @@
     return jnp.concatenate([high, high, low], axis=0)
 
 
-def tile_kernel(tile, halo, left, right, band_rows, band_cols, spectrum, inverse_rms):
+def tile_kernel(tile, halo, band_rows, band_cols, right, left, spectrum, inverse_rms):
     layers, rows, columns = tile.shape
     e = halo.shape[1]
     blocks = [[tile[l, b * e : (b + 1) * e, :] for b in range(3)] + [halo[l]] for l in range(layers)]
+    squares = [sum(blocks[l][b] * blocks[l][b] for l in range(layers)) for b in range(4)]
+    parts = [split(v) for v in squares]
+    for b in range(3):
+        tall = jnp.concatenate([parts[b][0], parts[b + 1][0], parts[b][1], parts[b + 1][1]], axis=0)
+        summed = dot(band_rows[...], tall)
+        high, low = split(summed)
+        for c in range(3):
+            pair = (high[:, c * e : (c + 2) * e], low[:, c * e : (c + 2) * e])
+            if c < 2:
+                energy = dot(jnp.concatenate(pair, axis=1), band_cols[...])
+            else:
+                energy = dot(pair[0], band_cols[:e, :]) + dot(pair[1], band_cols[:e, :])
+            inverse_rms[b * e : (b + 1) * e, c * e : (c + 1) * e] = lax.rsqrt(
+                energy * (1.0 / (layers * e * e)) + 1e-05
+            )
     for l in range(layers):
         a0, a1, a2, a3 = blocks[l]
         for si, s in enumerate(SIGNS):
@@ -97,30 +115,19 @@
                 spectrum[l, 1, place, lanes] = -(cs + sc)
                 spectrum[l, 2, place, lanes] = cc + ss
                 spectrum[l, 3, place, lanes] = sc - cs
-    squares = [sum(blocks[l][b] * blocks[l][b] for l in range(layers)) for b in range(4)]
-    parts = [split(v) for v in squares]
-    for b in range(3):
-        tall = jnp.concatenate([parts[b][0], parts[b + 1][0], parts[b][1], parts[b + 1][1]], axis=0)
-        summed = dot(band_rows[...], tall)
-        high, low = split(summed)
-        for c in range(3):
-            pair = (high[:, c * e : (c + 2) * e], low[:, c * e : (c + 2) * e])
-            if c < 2:
-                energy = dot(jnp.concatenate(pair, axis=1), band_cols[...])
-            else:
-                energy = dot(pair[0], band_cols[:e, :]) + dot(pair[1], band_cols[:e, :])
-            inverse_rms[b * e : (b + 1) * e, c * e : (c + 1) * e] = lax.rsqrt(
-                energy * (1.0 / (layers * e * e)) + 1e-05
-            )
-
-
-def score_kernel(
-    slots, order, clip, spectrum, inverse_rms, clip_left, clip_right, back_left, back_right, *rest
+
+
+def score_clip(
+    order, clip, spectrum, inverse_rms, clip_left, clip_right, back_left, back_right, scores
 ):
-    scores, peaks = rest[-2:]
     layers, e, _ = clip.shape
     root = math.sqrt(layers * e * e)
-    first = [clip[order[l]] for l in range(layers)]
+    first = []
+    for l in range(layers):
+        matched = clip[0]
+        for m in range(1, layers):
+            matched = jnp.where(order[l : l + 1, :] == m, clip[m], matched)
+        first.append(matched)
     total = sum(jnp.sum(v * v, keepdims=True) for v in first)
     scale = lax.rsqrt(total * (1.0 / (layers * e * e)) + 1e-05) * (1.0 / root)
     along = dot(beside(jnp.concatenate(first, axis=0)), clip_right[...])
@@ -161,75 +168,152 @@
     b1 = SIGNS[0] * (p[:, e:] + m[:, e:]) + (p[:, :e] - m[:, :e])
     result = jnp.concatenate([b0, b1, b2], axis=1) * inverse_rms[...] * scale
     scores[...] = result
-    largest = jnp.max(result)
-    i = pl.program_id(0)
-
-    @pl.when(i == 0)
-    def _():
-        peaks[...] = jnp.full(peaks.shape, -jnp.inf, jnp.float32)
-
-    row = lax.broadcasted_iota(jnp.int32, peaks.shape, 0)
-    peaks[...] = jnp.where(row == slots[i], largest, peaks[...])
-
-
-def whole(array):
-    return pl.BlockSpec(array.shape, lambda *_: (0,) * array.ndim)
-
-
-def tile_call(tiles, halo, consts):
+    return jnp.max(result)
+
+
+OUTSIDE = pl.BlockSpec(memory_space=pltpu.HBM)
+INSIDE = pl.BlockSpec(memory_space=pltpu.VMEM)
+
+
+def pick_call(block_owner, block_clips, layer_order, library, tiles, bits):
+    _, layers, e, _ = library.shape
+    blocks, per_block = block_clips.shape
+
+    def kernel(owner_in, clips_in, order_in, library, tiles, *refs):
+        mine, theirs, edge, owner_bits, order, owner, clips, layer, sems = refs
+        small = [
+            pltpu.make_async_copy(source, target, sems.at[i])
+            for i, (source, target) in enumerate(
+                ((clips_in, clips), (owner_in, owner), (order_in, layer))
+            )
+        ]
+        for copy in small:
+            copy.start()
+        rows = [
+            pltpu.make_async_copy(tiles.at[l, pl.ds(0, e), :], edge.at[l], sems.at[5 + l])
+            for l in range(layers)
+        ]
+        for copy in rows:
+            copy.start()
+        me, block = lax.axis_index("tile"), lax.axis_index("groups") % 2
+        core = me % 2
+        small[0].wait()
+        large = [
+            pltpu.make_async_copy(library.at[clips[block, core]], mine, sems.at[3]),
+            pltpu.make_async_copy(library.at[clips[block, 1 - core]], theirs, sems.at[4]),
+        ]
+        for copy in large:
+            copy.start()
+        small[1].wait()
+        small[2].wait()
+        differ = owner[block] ^ me
+        row = lax.broadcasted_iota(jnp.int32, owner_bits.shape, 0)
+        value = jnp.zeros(owner_bits.shape, jnp.int32)
+        for k in range(bits):
+            value = jnp.where(row == k, (differ >> k) & 1, value)
+        owner_bits[...] = value
+        value = jnp.zeros(owner_bits.shape, jnp.int32)
+        for l in range(layers):
+            value = jnp.where(row == l, layer[0, l], value)
+        order[...] = value
+        for copy in large + rows:
+            copy.wait()
+
+    clip = jax.ShapeDtypeStruct((layers, e, e), jnp.float32)
+    edge = jax.ShapeDtypeStruct((layers, e, tiles.shape[-1]), jnp.float32)
+    table = jax.ShapeDtypeStruct((8, e), jnp.int32)
+    return pl.pallas_call(
+        kernel,
+        out_shape=(clip, clip, edge, table, table),
+        in_specs=[OUTSIDE] * 5,
+        out_specs=(INSIDE,) * 5,
+        scratch_shapes=[
+            pltpu.SMEM(block_owner.shape, jnp.int32),
+            pltpu.SMEM(block_clips.shape, jnp.int32),
+            pltpu.SMEM(layer_order.shape, jnp.int32),
+            pltpu.SemaphoreType.DMA((5 + layers,)),
+        ],
+        compiler_params=pltpu.CompilerParams(vmem_limit_bytes=WHOLE),
+    )(block_owner, block_clips, layer_order, library, tiles)
+
+
+def tile_call(tiles, halo, own):
     layers, rows, columns = tiles.shape
     e = halo.shape[1]
-    args = (tiles, halo) + consts
     return pl.pallas_call(
         tile_kernel,
+        in_specs=[INSIDE] * (2 + len(own)),
+        out_specs=(INSIDE, INSIDE),
         out_shape=(
             jax.ShapeDtypeStruct((layers, 4, 2 * e, 2 * e), jnp.float32),
             jax.ShapeDtypeStruct((rows, columns), jnp.float32),
         ),
-        compiler_params=pltpu.CompilerParams(vmem_limit_bytes=48 * 1024 * 1024),
+        compiler_params=pltpu.CompilerParams(vmem_limit_bytes=MOST),
         cost_estimate=pl.CostEstimate(flops=2_000_000_000, bytes_accessed=6_000_000, transcendentals=0),
-    )(*args)
-
-
-def score_call(slots, order, clips, spectrum, inverse_rms, consts, count, before):
-    n, layers, e, _ = clips.shape
+    )(tiles, halo, *own)
+
+
+def score_call(first, clips, order, spectrum, inverse_rms, consts, count, before):
+    n = len(clips)
+    layers, e, _ = clips[0].shape
     rows, columns = inverse_rms.shape
-    fixed = (spectrum, inverse_rms) + consts
-    in_specs = [pl.BlockSpec((None, layers, e, e), lambda i, *_: (i, 0, 0, 0))]
-    in_specs += [whole(a) for a in fixed]
-    args = (clips,) + fixed
+    args = (*clips, order, spectrum, inverse_rms, *consts)
+    in_specs = [INSIDE] * len(args)
     aliases = {}
     if before is not None:
-        in_specs.append(pl.BlockSpec(memory_space=pl.ANY))
+        in_specs.append(OUTSIDE)
+        aliases = {len(args): 0}
         args += (before,)
-        aliases = {2 + len(args) - 1: 0}
+
+    def kernel(*refs):
+        scores, peaks, result, sems = refs[-4:]
+        order, *rest = refs[n : n + 7]
+        own = lax.axis_index("groups") % 2 * 2 + lax.axis_index("tile") % 2
+        slots = [own ^ (first + i) for i in range(n)]
+        row = lax.broadcasted_iota(jnp.int32, peaks.shape, 0)
+        best = jnp.full(peaks.shape, -jnp.inf, jnp.float32)
+        copies = []
+        for i in range(n):
+            if i > 1:
+                copies[i - 2].wait()
+            largest = score_clip(order, refs[i], *rest, result.at[i % 2])
+            best = jnp.where(row == slots[i], largest, best)
+            copies.append(pltpu.make_async_copy(result.at[i % 2], scores.at[slots[i]], sems.at[i % 2]))
+            copies[i].start()
+        peaks[...] = best
+        for copy in copies[-2:]:
+            copy.wait()
+
     return pl.pallas_call(
-        score_kernel,
-        grid_spec=pltpu.PrefetchScalarGridSpec(
-            num_scalar_prefetch=2,
-            grid=(n,),
-            in_specs=in_specs,
-            out_specs=(
-                pl.BlockSpec((None, rows, columns), lambda i, slots, order: (slots[i], 0, 0)),
-                pl.BlockSpec((8, 128), lambda i, *_: (0, 0)),
-            ),
-        ),
+        kernel,
+        in_specs=in_specs,
+        out_specs=(OUTSIDE, INSIDE),
         out_shape=(
             jax.ShapeDtypeStruct((count, rows, columns), jnp.float32),
             jax.ShapeDtypeStruct((8, 128), jnp.float32),
         ),
+        scratch_shapes=[
+            pltpu.VMEM((2, rows, columns), jnp.float32),
+            pltpu.SemaphoreType.DMA((2,)),
+        ],
         input_output_aliases=aliases,
-        compiler_params=pltpu.CompilerParams(
-            vmem_limit_bytes=56 * 1024 * 1024, dimension_semantics=("arbitrary",)
-        ),
+        compiler_params=pltpu.CompilerParams(vmem_limit_bytes=VMEM),
         cost_estimate=pl.CostEstimate(
             flops=n * 1_300_000_000, bytes_accessed=6_000_000, transcendentals=0
         ),
-    )(slots, order, *args)
+    )(*args)
 
 
 def swap(block, axis, distance):
     return lax.ppermute(block, axis, [(i, i ^ distance) for i in range(lax.axis_size(axis))])
+
+
+def cross_swap(block):
+    groups, devices = lax.axis_size("groups"), lax.axis_size("tile")
+    route = [
+        (g * devices + i, (g ^ 1) * devices + (i ^ 1)) for g in range(groups) for i in range(devices)
+    ]
+    return lax.ppermute(block, ("groups", "tile"), route)
 
 
 def local(tiles, library, block_owner, block_clips, layer_order):
@@ -242,39 +326,35 @@
     tile_left, tile_right, clip_left, clip_right, back_left, back_right = map(jnp.asarray, factors(e))
     band_rows, band_cols = map(jnp.asarray, bands(e))
 
-    me = lax.axis_index("tile")
-    core = me % 2
-    block = lax.axis_index("groups") % 2
-    owner = block_owner[block]
-    chosen = lax.dynamic_index_in_dim(block_clips, block, 0, keepdims=False)
-    mine = lax.dynamic_index_in_dim(library, chosen[core], 0, keepdims=False)
-    theirs = lax.dynamic_index_in_dim(library, chosen[1 - core], 0, keepdims=False)
-    differ = owner ^ me
-    got = swap(theirs, "tile", 1)
-    held = jnp.where((differ & 1) == 0, mine, got)
-    distance = 2
-    while distance < devices:
-        got = swap(held, "tile", distance)
-        held = jnp.where((differ & distance) == 0, held, got)
-        distance *= 2
+    bits = devices.bit_length() - 1
+    mine, theirs, edge, differ, order = pick_call(
+        block_owner, block_clips, layer_order, library, tiles, bits
+    )
+    own = (band_rows, band_cols, tile_right, tile_left)
+    edge, tiles, own = lax.optimization_barrier((edge, tiles, own))
+    halo = lax.ppermute(edge, "tile", [(i, i - 1) for i in range(1, devices)])
+
+    def take(k, own, got):
+        return jnp.where(differ[k][None, None, :] == 0, own, got)
+
+    held = take(0, mine, swap(theirs, "tile", 1))
+    consts = (clip_left, clip_right, back_left, back_right)
+    for k in range(1, bits):
+        got = swap(held, "tile", 1 << k)
+        if k == 2:
+            got, halo = lax.optimization_barrier((got, halo))
+            spectrum, inverse_rms = tile_call(tiles, halo, own)
+        held = take(k, held, got)
+        if k == 3:
+            held, spectrum, inverse_rms = lax.optimization_barrier((held, spectrum, inverse_rms))
+    twin = swap(held, "tile", 1)
     other = swap(held, "groups", 1)
-    rest = swap(jnp.stack([held, other]), "tile", 1)
-    later = jnp.concatenate([other[None], rest], axis=0)
-
-    route = [(i, i - 1) for i in range(1, devices)]
-    halo = lax.ppermute(tiles[:, :e, :], "tile", route)
-    spectrum, inverse_rms = tile_call(
-        tiles, halo, (tile_left, tile_right, band_rows, band_cols)
-    )
-    consts = (clip_left, clip_right, back_left, back_right)
-    order = layer_order[0]
+    cross = cross_swap(held)
     count = blocks * per_block
-    slot = block * per_block + core
-    first = slot[None].astype(jnp.int32)
-    second = jnp.stack([slot ^ 2, slot ^ 1, slot ^ 3]).astype(jnp.int32)
-    scores, peaks = score_call(first, order, held[None], spectrum, inverse_rms, consts, count, None)
-    scores, more = score_call(second, order, later, spectrum, inverse_rms, consts, count, scores)
-    best = jnp.maximum(peaks, more)
+    shared = (order, spectrum, inverse_rms, consts, count)
+    scores, best = score_call(0, (held, twin), *shared, None)
+    scores, more = score_call(2, (other, cross), *shared, scores)
+    best = jnp.maximum(best, more)
     distance = 1
     while distance < devices:
         best = jnp.maximum(best, swap(best, "tile", distance))

time: 77.3 us -> 55.8 us (0.72)
  local copies, waits for them, and re-layouts: 8.33 us -> 0.83 us
  between operations: 5.42 us -> 0.85 us
  Pallas kernels: 20.5 us -> 16.5 us
  other arithmetic: 5.78 us -> 1.82 us
  waiting for transfers between devices: 22.4 us -> 19.2 us
  starting transfers between devices: 14.5 us -> 16.4 us
    pallas_call x3 -> x4, Pallas kernels: 20.5 us -> 16.5 us  [the longest x2 10.3 us: score_call(): pl.pallas_call(kernel, in_specs=in_specs, out_specs=(OUTSIDE, INSIDE), ou...]
    ppermute x10, waiting for transfers between devices: 22.4 us -> 19.2 us  [swap(): lax.ppermute(block, axis, [(i, i ^ distance) for i in range(lax.axis_size...]
    dynamic_slice x2 -> x0, local copies, waits for them, and re-layouts: 2.68 us -> none  [the longest x1 1.44 us: local(): mine = lax.dynamic_index_in_dim(library, chosen[core], 0, keepdims=False)]
    unnamed x20, local copies, waits for them, and re-layouts: 2.19 us -> 0.06 us
    slice x1 -> x0, local copies, waits for them, and re-layouts: 1.77 us -> none  [local(): halo = lax.ppermute(tiles[:, :e, :], 'tile', route)]
    concatenate x1 -> x0, other arithmetic: 1.69 us -> none  [local(): later = jnp.concatenate([other[None], rest], axis=0)]
    ppermute x1 -> x2, starting transfers between devices: 1.28 us -> 2.89 us  [the longest x1 1.61 us: cross_swap(): return lax.ppermute(block, ('groups', 'tile'), route)]
    another operation x2 -> x0, other arithmetic: 1.52 us -> none  [the longest x1 0.92 us: local(): rest = swap(jnp.stack([held, other]), 'tile', 1)]
  transfers between devices with their start and end apart: 11 -> 12, of which waited for: 8 -> 9; matrix products, arithmetic and copies ran while one was open for 7% -> 2% of each run, Pallas kernels for 12% -> 15%
where the time goes in v1:
time: 55.8 us; the launch traced here: 55.6 us
  waiting for transfers between devices  19.2 us (34%)
  Pallas kernels  16.5 us (30%)
  starting transfers between devices  16.4 us (29%)
  other arithmetic  1.82 us (3%)
  between operations  0.85 us (2%)
  local copies, waits for them, and re-layouts  0.83 us (1%)
    ppermute x10, waiting for transfers between devices, swap(): lax.ppermute(block, axis, [(i, i ^ distance) for i in range(lax.axis_size...  19.2 us
    ppermute x10, starting transfers between devices, swap(): lax.ppermute(block, axis, [(i, i ^ distance) for i in range(lax.axis_size...  13.5 us
    pallas_call x2, Pallas kernels, score_call(): pl.pallas_call(kernel, in_specs=in_specs, out_specs=(OUTSIDE, INSIDE), ou...  10.3 us
    pallas_call x1, Pallas kernels, tile_call(): pl.pallas_call(tile_kernel, in_specs=[INSIDE] * (2 + len(own)), out_specs...  3.16 us
    pallas_call x1, Pallas kernels, pick_call(): pl.pallas_call(kernel, out_shape=(clip, clip, edge, table, table), in_spe...  3 us
    ppermute x1, starting transfers between devices, cross_swap(): return lax.ppermute(block, ('groups', 'tile'), route)  1.61 us
    ppermute x1, starting transfers between devices, local(): halo = lax.ppermute(edge, 'tile', [(i, i - 1) for i in range(1, devices)])  1.28 us
  transfers between devices with their start and end apart: 12, of which 9 were waited for; matrix products, arithmetic and copies ran while one was open for 2% of the time, Pallas kernels for 15%

profile of v1, /device:TPU:0, one launch (start us, length us, event | category | flops | bytes accessed | tf_op | source)
XLA Modules:
  0.0 55.6 jit_solution(5481170875615141244)
XLA Ops:
  0.6 0.0 copy-start.8
  0.6 0.0 copy-start.9
  0.7 0.0 copy-start.4
  0.7 0.0 copy-start.5
  0.7 0.0 copy-start
  0.7 3.0 %shard_map.140 = (f32[2,128,128]{2,1,0:T(8,128)}, f32[2,128,128]{2,1,0:T(8,128)}, f32[2,128,384]{2,1,0:T(8,128)}, s32[8,128]{1,0:T(8,128)}, s32[8,128]{1,0:T(8,128)}) custom-call(s32[2]{0:T(128)} %owner_in.1, s32[2,2]{1,0:T(2,128)} %clips_in.1, s32[1,2]{1,0:T(1,128)} %order_in.1, f32[8,2,128,128]{3,2,1,0:T(8,128)} %library.1, f32[2,384,384]{2,1,0:T(8,128)} %tile), custom_call_target="tpu_custom_call" | custom-call | tf_op jit(solution)/shard_map/pallas_call | solution.py:225
  3.7 0.5 collective-permute-start
  4.2 0.8 %compare_bitcast_fusion.3 = (pred[128]{0:T(512)(128)(4,1)S(1)}, pred[128]{0:T(512)(128)(4,1)S(1)}, pred[128]{0:T(512)(128)(4,1)S(1)}, pred[128]{0:T(512)(128)(4,1)S(1)}) fusion(s32[8,128]{1,0:T(8,128)} %get-tuple-element.24), kind=kLoop, calls=%fused_computation.8 | loop fusion | flops 512 | bytes 2560 | tf_op jit(solution)/shard_map/eq | solution.py:338
  5.1 0.4 collective-permute-done
  5.4 0.9 %broadcast_select_fusion = f32[2,128,128]{2,1,0:T(8,128)S(1)} fusion(f32[2,128,128]{2,1,0:T(8,128)} %get-tuple-element.25, f32[2,128,128]{2,1,0:T(8,128)S(1)} %collective-permute-done, pred[128]{0:T(512)(128)(4,1)S(1)} %get-tuple-element.47), kind=kLoop, calls=%fused_computation | loop fusion | flops 32768 | bytes 393344 | tf_op jit(solution)/shard_map/jit(_where)/select_n | solution.py:338
  6.3 2.9 %collective-permute-start.1 = (f32[2,128,128]{2,1,0:T(8,128)S(1)}, f32[2,128,128]{2,1,0:T(8,128)S(1)}, u32[]{:S(2)}, u32[]{:S(2)}) collective-permute-start(f32[2,128,128]{2,1,0:T(8,128)S(1)} %broadcast_select_fusion), channel_id=1, source_target_pairs={{0,2},{1,3},{2,0},{3,1},{4,6},{5,7},{6,4},{7,5},{8,10},{9,11},{10,... | collective-permute-start | bytes 393224 | tf_op jit(solution)/shard_map/ppermute | solution.py:308
  9.3 1.3 %collective-permute-start.3 = (f32[2,128,384]{2,1,0:T(8,128)}, f32[2,128,384]{2,1,0:T(8,128)S(1)}, u32[]{:S(2)}, u32[]{:S(2)}) collective-permute-start(f32[2,128,384]{2,1,0:T(8,128)} %get-tuple-element.28), channel_id=1, source_target_pairs={{1,0},{2,1},{3,2},{4,3},{5,4},{6,5},{7,6},{8,7},{9,8},{10,9},{11,1... | collective-permute-start | bytes 1179656 | tf_op jit(solution)/shard_map/ppermute | solution.py:335
  10.6 2.5 %collective-permute-done.1 = f32[2,128,128]{2,1,0:T(8,128)S(1)} collective-permute-done((f32[2,128,128]{2,1,0:T(8,128)S(1)}, f32[2,128,128]{2,1,0:T(8,128)S(1)}, u32[]{:S(2)}, u32[]{:S(2)}) %collective-permute-start.1) | collective-permute-done | bytes 131104 | tf_op jit(solution)/shard_map/ppermute | solution.py:308
  13.1 1.9 %collective-permute-start.2 = (f32[2,128,128]{2,1,0:T(8,128)S(1)}, f32[2,128,128]{2,1,0:T(8,128)S(1)}, u32[]{:S(2)}, u32[]{:S(2)}) collective-permute-start(f32[2,128,128]{2,1,0:T(8,128)S(1)} %broadcast_select_fusion.1), channel_id=1, source_target_pairs={{0,4},{1,5},{2,6},{3,7},{4,0},{5,1},{6,2},{7,3},{8,12},{9,13},{10,... | collective-permute-start | bytes 393224 | tf_op jit(solution)/shard_map/ppermute | solution.py:308
  15.0 6.5 %collective-permute-done.2 = f32[2,128,128]{2,1,0:T(8,128)S(1)} collective-permute-done((f32[2,128,128]{2,1,0:T(8,128)S(1)}, f32[2,128,128]{2,1,0:T(8,128)S(1)}, u32[]{:S(2)}, u32[]{:S(2)}) %collective-permute-start.2) | collective-permute-done | bytes 131104 | tf_op jit(solution)/shard_map/ppermute | solution.py:308
  21.5 0.0 collective-permute-done.3.halo
  21.5 0.0 copy-start.1
  21.5 0.0 copy-start.2
  21.6 0.0 copy-start.3
  21.6 0.0 copy-start.6
  21.6 0.0 copy-start.7
  21.6 3.0 %collective-permute-start.4 = (f32[2,128,128]{2,1,0:T(8,128)S(1)}, f32[2,128,128]{2,1,0:T(8,128)S(1)}, u32[]{:S(2)}, u32[]{:S(2)}) collective-permute-start(f32[2,128,128]{2,1,0:T(8,128)S(1)} %broadcast_select_fusion.2), channel_id=1, source_target_pairs={{0,8},{1,9},{2,10},{3,11},{4,12},{5,13},{6,14},{7,15},{8,0},{9,1},... | collective-permute-start | bytes 393224 | tf_op jit(solution)/shard_map/ppermute | solution.py:308
  24.6 0.0 copy-done.8
  24.6 0.0 copy-done.9
  24.6 0.0 copy-done.4
  24.6 0.0 copy-done.5
  24.6 0.0 copy-done
  24.6 3.2 %shard_map.141 = (f32[2,4,256,256]{3,2,1,0:T(8,128)S(1)}, f32[384,384]{1,0:T(8,128)S(1)}) custom-call(f32[2,384,384]{2,1,0:T(8,128)S(1)} %copy-done, f32[2,128,384]{2,1,0:T(8,128)S(1)} %collective-permute-done.3.halo, bf16[128,512]{1,0:T(8,128)(2,1)S(1)} %copy-done.9, bf16[512,128]{1,0:T(8,128)(2,1)S(1)} %copy-done.8, bf16[2,768,256]{2,1,0:T(8,128)(2,1)S(1)} %copy-done.4, ...), custom_call_target="tpu_custom_call" | custom-call | flops 2000000000 | bytes 6000000 | tf_op jit(solution)/shard_map/pallas_call | solution.py:243
  27.8 0.1 collective-permute-done.4
  28.0 0.1 collective-permute-start.7
  28.0 1.6 %collective-permute-start.6 = (f32[2,128,128]{2,1,0:T(8,128)S(1)}, f32[2,128,128]{2,1,0:T(8,128)S(1)}, u32[]{:S(2)}, u32[]{:S(2)}) collective-permute-start(f32[2,128,128]{2,1,0:T(8,128)S(1)} %broadcast_select_fusion.3.refs_0_), channel_id=1, source_target_pairs={{0,17},{1,16},{2,19},{3,18},{4,21},{5,20},{6,23},{7,22},{8,25},{9,... | collective-permute-start | bytes 393224 | tf_op jit(solution)/shard_map/ppermute | solution.py:316
  29.6 0.5 collective-permute-start.5
  30.2 0.0 collective-permute-done.7.refs_1_
  30.2 0.0 copy-done.1
  30.2 0.0 copy-done.2
  30.2 0.0 copy-done.3
  30.2 0.0 copy-done.6
  30.2 0.0 copy-done.7
  30.2 5.2 %shard_map.142 = (f32[4,384,384]{2,1,0:T(8,128)}, f32[8,128]{1,0:T(8,128)S(1)}) custom-call(f32[2,128,128]{2,1,0:T(8,128)S(1)} %broadcast_select_fusion.3.refs_0_, f32[2,128,128]{2,1,0:T(8,128)S(1)} %collective-permute-done.7.refs_1_, s32[8,128]{1,0:T(8,128)S(1)} %copy-done.1, f32[2,4,256,256]{3,2,1,0:T(8,128)S(1)} %get-tuple-element.40.refs_3_, ...), custom_call_target="tpu_custom_call" | custom-call | flops 2600000000 | bytes 6000000 | tf_op jit(solution)/shard_map/pallas_call | solution.py:287
  35.4 0.0 collective-permute-done.6.refs_1_
  35.4 1.3 %collective-permute-done.5.refs_0_ = f32[2,128,128]{2,1,0:T(8,128)S(1)} collective-permute-done((f32[2,128,128]{2,1,0:T(8,128)S(1)}, f32[2,128,128]{2,1,0:T(8,128)S(1)}, u32[]{:S(2)}, u32[]{:S(2)}) %collective-permute-start.5) | collective-permute-done | bytes 131104 | tf_op jit(solution)/shard_map/ppermute | solution.py:308
  36.7 5.2 %shard_map.143 = (f32[4,384,384]{2,1,0:T(8,128)}, f32[8,128]{1,0:T(8,128)S(1)}) custom-call(f32[2,128,128]{2,1,0:T(8,128)S(1)} %collective-permute-done.5.refs_0_, f32[2,128,128]{2,1,0:T(8,128)S(1)} %collective-permute-done.6.refs_1_, s32[8,128]{1,0:T(8,128)S(1)} %copy-done.1, ...), custom_call_target="tpu_custom_call", output_to_operand_aliasing={{0}: (9, {})} | custom-call | flops 2600000000 | bytes 6000000 | tf_op jit(solution)/shard_map/pallas_call | solution.py:287
  41.9 0.1 collective-permute-start.8
  42.0 1.2 %collective-permute-done.8 = f32[8,128]{1,0:T(8,128)S(1)} collective-permute-done((f32[8,128]{1,0:T(8,128)S(1)}, f32[8,128]{1,0:T(8,128)S(1)}, u32[]{:S(2)}, u32[]{:S(2)}) %collective-permute-start.8) | collective-permute-done | bytes 4128 | tf_op jit(solution)/shard_map/ppermute | solution.py:308
  43.1 2.0 %collective-permute-start.9 = (f32[8,128]{1,0:T(8,128)S(1)}, f32[8,128]{1,0:T(8,128)S(1)}, u32[]{:S(2)}, u32[]{:S(2)}) collective-permute-start(f32[8,128]{1,0:T(8,128)S(1)} %max.16), channel_id=1, source_target_pairs={{0,2},{1,3},{2,0},{3,1},{4,6},{5,7},{6,4},{7,5},{8,10},{9,11},{10,... | collective-permute-start | bytes 12296 | tf_op jit(solution)/shard_map/ppermute | solution.py:308
  45.1 1.6 %collective-permute-done.9 = f32[8,128]{1,0:T(8,128)S(1)} collective-permute-done((f32[8,128]{1,0:T(8,128)S(1)}, f32[8,128]{1,0:T(8,128)S(1)}, u32[]{:S(2)}, u32[]{:S(2)}) %collective-permute-start.9) | collective-permute-done | bytes 4128 | tf_op jit(solution)/shard_map/ppermute | solution.py:308
  46.7 0.0 collective-permute-start.10
  46.7 3.6 %collective-permute-done.10 = f32[8,128]{1,0:T(8,128)S(1)} collective-permute-done((f32[8,128]{1,0:T(8,128)S(1)}, f32[8,128]{1,0:T(8,128)S(1)}, u32[]{:S(2)}, u32[]{:S(2)}) %collective-permute-start.10) | collective-permute-done | bytes 4128 | tf_op jit(solution)/shard_map/ppermute | solution.py:308
  50.3 2.5 %collective-permute-start.11 = (f32[8,128]{1,0:T(8,128)S(1)}, f32[8,128]{1,0:T(8,128)S(1)}, u32[]{:S(2)}, u32[]{:S(2)}) collective-permute-start(f32[8,128]{1,0:T(8,128)S(1)} %max.18), channel_id=1, source_target_pairs={{0,8},{1,9},{2,10},{3,11},{4,12},{5,13},{6,14},{7,15},{8,0},{9,1},... | collective-permute-start | bytes 12296 | tf_op jit(solution)/shard_map/ppermute | solution.py:308
  52.9 2.0 %collective-permute-done.11 = f32[8,128]{1,0:T(8,128)S(1)} collective-permute-done((f32[8,128]{1,0:T(8,128)S(1)}, f32[8,128]{1,0:T(8,128)S(1)}, u32[]{:S(2)}, u32[]{:S(2)}) %collective-permute-start.11) | collective-permute-done | bytes 4128 | tf_op jit(solution)/shard_map/ppermute | solution.py:308
  54.9 0.1 slice_reduce_fusion
  55.0 0.6 %reshape_squeeze.3 = f32[2,2]{1,0:T(2,128)} reshape(f32[4]{0:T(128)S(1)} %slice_reduce_fusion) | data formatting | bytes 32 | tf_op jit(solution)/shard_map/reshape;squeeze | solution.py:364
  (8 shorter events, 0.1 us)
Async XLA Ops:
  0.6 24.0 %copy-start.8 = (bf16[512,128]{1,0:T(8,128)(2,1)S(1)}, bf16[512,128]{1,0:T(8,128)(2,1)}, u32[]{:S(2)}) copy-start(bf16[512,128]{1,0:T(8,128)(2,1)} %constant.25.clone.band_cols) | copy-start | bytes 393220
  0.6 24.0 %copy-start.9 = (bf16[128,512]{1,0:T(8,128)(2,1)S(1)}, bf16[128,512]{1,0:T(8,128)(2,1)}, u32[]{:S(2)}) copy-start(bf16[128,512]{1,0:T(8,128)(2,1)} %constant.24.clone.band_rows) | copy-start | bytes 393220
  0.7 24.0 %copy-start.4 = (bf16[2,768,256]{2,1,0:T(8,128)(2,1)S(1)}, bf16[2,768,256]{2,1,0:T(8,128)(2,1)}, u32[]{:S(2)}) copy-start(bf16[2,768,256]{2,1,0:T(8,128)(2,1)} %constant.19.clone.right) | copy-start | bytes 2359300
  0.7 23.9 %copy-start.5 = (bf16[2,256,768]{2,1,0:T(8,128)(2,1)S(1)}, bf16[2,256,768]{2,1,0:T(8,128)(2,1)}, u32[]{:S(2)}) copy-start(bf16[2,256,768]{2,1,0:T(8,128)(2,1)} %constant.18.clone.left) | copy-start | bytes 2359300
  0.7 23.9 %copy-start = (f32[2,384,384]{2,1,0:T(8,128)S(1)}, f32[2,384,384]{2,1,0:T(8,128)}, u32[]{:S(2)}) copy-start(f32[2,384,384]{2,1,0:T(8,128)} %tile) | copy-start | bytes 3538948
  3.7 1.7 %collective-permute-start = (f32[2,128,128]{2,1,0:T(8,128)}, f32[2,128,128]{2,1,0:T(8,128)S(1)}, u32[]{:S(2)}, u32[]{:S(2)}) collective-permute-start(f32[2,128,128]{2,1,0:T(8,128)} %get-tuple-element.26), channel_id=1, source_target_pairs={{0,1},{1,0},{2,3},{3,2},{4,5},{5,4},{6,7},{7,6},{8,9},{9,8},{10,11... | collective-permute-start | bytes 393224 | tf_op jit(solution)/shard_map/ppermute | solution.py:308
  6.3 6.8 %collective-permute-start.1 = (f32[2,128,128]{2,1,0:T(8,128)S(1)}, f32[2,128,128]{2,1,0:T(8,128)S(1)}, u32[]{:S(2)}, u32[]{:S(2)}) collective-permute-start(f32[2,128,128]{2,1,0:T(8,128)S(1)} %broadcast_select_fusion), channel_id=1, source_target_pairs={{0,2},{1,3},{2,0},{3,1},{4,6},{5,7},{6,4},{7,5},{8,10},{9,11},{10,... | collective-permute-start | bytes 393224 | tf_op jit(solution)/shard_map/ppermute | solution.py:308
  9.3 12.2 %collective-permute-start.3 = (f32[2,128,384]{2,1,0:T(8,128)}, f32[2,128,384]{2,1,0:T(8,128)S(1)}, u32[]{:S(2)}, u32[]{:S(2)}) collective-permute-start(f32[2,128,384]{2,1,0:T(8,128)} %get-tuple-element.28), channel_id=1, source_target_pairs={{1,0},{2,1},{3,2},{4,3},{5,4},{6,5},{7,6},{8,7},{9,8},{10,9},{11,1... | collective-permute-start | bytes 1179656 | tf_op jit(solution)/shard_map/ppermute | solution.py:335
  13.1 8.4 %collective-permute-start.2 = (f32[2,128,128]{2,1,0:T(8,128)S(1)}, f32[2,128,128]{2,1,0:T(8,128)S(1)}, u32[]{:S(2)}, u32[]{:S(2)}) collective-permute-start(f32[2,128,128]{2,1,0:T(8,128)S(1)} %broadcast_select_fusion.1), channel_id=1, source_target_pairs={{0,4},{1,5},{2,6},{3,7},{4,0},{5,1},{6,2},{7,3},{8,12},{9,13},{10,... | collective-permute-start | bytes 393224 | tf_op jit(solution)/shard_map/ppermute | solution.py:308
  21.5 8.6 %copy-start.1 = (s32[8,128]{1,0:T(8,128)S(1)}, s32[8,128]{1,0:T(8,128)}, u32[]{:S(2)}) copy-start(s32[8,128]{1,0:T(8,128)} %get-tuple-element.39.refs_2_) | copy-start | bytes 12292
  21.5 8.6 %copy-start.2 = (bf16[2,768,256]{2,1,0:T(8,128)(2,1)S(1)}, bf16[2,768,256]{2,1,0:T(8,128)(2,1)}, u32[]{:S(2)}) copy-start(bf16[2,768,256]{2,1,0:T(8,128)(2,1)} %constant.23.clone.refs_8_) | copy-start | bytes 2359300
  21.6 8.6 %copy-start.3 = (bf16[2,256,768]{2,1,0:T(8,128)(2,1)S(1)}, bf16[2,256,768]{2,1,0:T(8,128)(2,1)}, u32[]{:S(2)}) copy-start(bf16[2,256,768]{2,1,0:T(8,128)(2,1)} %constant.22.clone.refs_7_) | copy-start | bytes 2359300
  21.6 8.6 %copy-start.6 = (bf16[384,512]{1,0:T(8,128)(2,1)S(1)}, bf16[384,512]{1,0:T(8,128)(2,1)}, u32[]{:S(2)}) copy-start(bf16[384,512]{1,0:T(8,128)(2,1)} %constant.21.clone.refs_6_) | copy-start | bytes 1179652
  21.6 8.6 %copy-start.7 = (bf16[512,384]{1,0:T(8,128)(2,1)S(1)}, bf16[512,384]{1,0:T(8,128)(2,1)}, u32[]{:S(2)}) copy-start(bf16[512,384]{1,0:T(8,128)(2,1)} %constant.20.clone.refs_5_) | copy-start | bytes 1179652
  21.6 6.3 %collective-permute-start.4 = (f32[2,128,128]{2,1,0:T(8,128)S(1)}, f32[2,128,128]{2,1,0:T(8,128)S(1)}, u32[]{:S(2)}, u32[]{:S(2)}) collective-permute-start(f32[2,128,128]{2,1,0:T(8,128)S(1)} %broadcast_select_fusion.2), channel_id=1, source_target_pairs={{0,8},{1,9},{2,10},{3,11},{4,12},{5,13},{6,14},{7,15},{8,0},{9,1},... | collective-permute-start | bytes 393224 | tf_op jit(solution)/shard_map/ppermute | solution.py:308
  28.0 2.2 %collective-permute-start.7 = (f32[2,128,128]{2,1,0:T(8,128)S(1)}, f32[2,128,128]{2,1,0:T(8,128)S(1)}, u32[]{:S(2)}, u32[]{:S(2)}) collective-permute-start(f32[2,128,128]{2,1,0:T(8,128)S(1)} %broadcast_select_fusion.3.refs_0_), channel_id=1, source_target_pairs={{0,1},{1,0},{2,3},{3,2},{4,5},{5,4},{6,7},{7,6},{8,9},{9,8},{10,11... | collective-permute-start | bytes 393224 | tf_op jit(solution)/shard_map/ppermute | solution.py:308
  28.0 7.4 %collective-permute-start.6 = (f32[2,128,128]{2,1,0:T(8,128)S(1)}, f32[2,128,128]{2,1,0:T(8,128)S(1)}, u32[]{:S(2)}, u32[]{:S(2)}) collective-permute-start(f32[2,128,128]{2,1,0:T(8,128)S(1)} %broadcast_select_fusion.3.refs_0_), channel_id=1, source_target_pairs={{0,17},{1,16},{2,19},{3,18},{4,21},{5,20},{6,23},{7,22},{8,25},{9,... | collective-permute-start | bytes 393224 | tf_op jit(solution)/shard_map/ppermute | solution.py:316
  29.6 7.1 %collective-permute-start.5 = (f32[2,128,128]{2,1,0:T(8,128)S(1)}, f32[2,128,128]{2,1,0:T(8,128)S(1)}, u32[]{:S(2)}, u32[]{:S(2)}) collective-permute-start(f32[2,128,128]{2,1,0:T(8,128)S(1)} %broadcast_select_fusion.3.refs_0_), channel_id=1, source_target_pairs={{0,16},{16,0},{1,17},{17,1},{2,18},{18,2},{3,19},{19,3},{4,20},{20... | collective-permute-start | bytes 393224 | tf_op jit(solution)/shard_map/ppermute | solution.py:308
  41.9 1.2 %collective-permute-start.8 = (f32[8,128]{1,0:T(8,128)S(1)}, f32[8,128]{1,0:T(8,128)S(1)}, u32[]{:S(2)}, u32[]{:S(2)}) collective-permute-start(f32[8,128]{1,0:T(8,128)S(1)} %max.15), channel_id=1, source_target_pairs={{0,1},{1,0},{2,3},{3,2},{4,5},{5,4},{6,7},{7,6},{8,9},{9,8},{10,11... | collective-permute-start | bytes 12296 | tf_op jit(solution)/shard_map/ppermute | solution.py:308
  43.1 3.6 %collective-permute-start.9 = (f32[8,128]{1,0:T(8,128)S(1)}, f32[8,128]{1,0:T(8,128)S(1)}, u32[]{:S(2)}, u32[]{:S(2)}) collective-permute-start(f32[8,128]{1,0:T(8,128)S(1)} %max.16), channel_id=1, source_target_pairs={{0,2},{1,3},{2,0},{3,1},{4,6},{5,7},{6,4},{7,5},{8,10},{9,11},{10,... | collective-permute-start | bytes 12296 | tf_op jit(solution)/shard_map/ppermute | solution.py:308
  46.7 3.6 %collective-permute-start.10 = (f32[8,128]{1,0:T(8,128)S(1)}, f32[8,128]{1,0:T(8,128)S(1)}, u32[]{:S(2)}, u32[]{:S(2)}) collective-permute-start(f32[8,128]{1,0:T(8,128)S(1)} %max.17), channel_id=1, source_target_pairs={{0,4},{1,5},{2,6},{3,7},{4,0},{5,1},{6,2},{7,3},{8,12},{9,13},{10,... | collective-permute-start | bytes 12296 | tf_op jit(solution)/shard_map/ppermute | solution.py:308
  50.3 4.5 %collective-permute-start.11 = (f32[8,128]{1,0:T(8,128)S(1)}, f32[8,128]{1,0:T(8,128)S(1)}, u32[]{:S(2)}, u32[]{:S(2)}) collective-permute-start(f32[8,128]{1,0:T(8,128)S(1)} %max.18), channel_id=1, source_target_pairs={{0,8},{1,9},{2,10},{3,11},{4,12},{5,13},{6,14},{7,15},{8,0},{9,1},... | collective-permute-start | bytes 12296 | tf_op jit(solution)/shard_map/ppermute | solution.py:308

commit v2 on v1

--- a/solution.py
+++ b/solution.py
@@ -12,7 +12,7 @@
 SIGNS = (math.sqrt(2.0), -math.sqrt(2.0))
 VMEM = 20 * 1024 * 1024
 MOST = 40 * 1024 * 1024
-WHOLE = 57 * 1024 * 1024
+WHOLE = 8 * 1024 * 1024
 
 
 def halves(matrix):
@@ -130,8 +130,10 @@
         first.append(matched)
     total = sum(jnp.sum(v * v, keepdims=True) for v in first)
     scale = lax.rsqrt(total * (1.0 / (layers * e * e)) + 1e-05) * (1.0 / root)
-    along = dot(beside(jnp.concatenate(first, axis=0)), clip_right[...])
-    both = [dot(clip_left[...], stacked(along[l * e : (l + 1) * e])) for l in range(layers)]
+    down = dot(clip_left[...], stacked(jnp.concatenate(first, axis=1)))
+    both = [
+        dot(beside(down[:, l * e : (l + 1) * e]), clip_right[...]) for l in range(layers)
+    ]
     rows = []
     for si in range(2):
         upper, lower = [], []
@@ -219,9 +221,11 @@
         for copy in large + rows:
             copy.wait()
 
-    clip = jax.ShapeDtypeStruct((layers, e, e), jnp.float32)
-    edge = jax.ShapeDtypeStruct((layers, e, tiles.shape[-1]), jnp.float32)
-    table = jax.ShapeDtypeStruct((8, e), jnp.int32)
+    clip = pltpu.VMEM((layers, e, e), jnp.float32)
+    edge = pltpu.VMEM((layers, e, tiles.shape[-1]), jnp.float32)
+    table = pltpu.VMEM((8, e), jnp.int32)
+    args = (block_owner, block_clips, layer_order, library, tiles)
+    args = [pltpu.with_memory_space_constraint(a, pltpu.HBM) for a in args]
     return pl.pallas_call(
         kernel,
         out_shape=(clip, clip, edge, table, table),
@@ -234,7 +238,32 @@
             pltpu.SemaphoreType.DMA((5 + layers,)),
         ],
         compiler_params=pltpu.CompilerParams(vmem_limit_bytes=WHOLE),
-    )(block_owner, block_clips, layer_order, library, tiles)
+    )(*args)
+
+
+def hold_call(arrays):
+    n = len(arrays)
+
+    def kernel(*refs):
+        copies = [
+            pltpu.make_async_copy(refs[i], refs[n + i], refs[-1].at[i]) for i in range(n)
+        ]
+        for copy in copies:
+            copy.start()
+        for copy in copies:
+            copy.wait()
+
+    return pl.pallas_call(
+        kernel,
+        out_shape=tuple(pltpu.VMEM(a.shape, a.dtype) for a in arrays),
+        in_specs=[OUTSIDE] * n,
+        out_specs=(INSIDE,) * n,
+        scratch_shapes=[pltpu.SemaphoreType.DMA((n,))],
+        compiler_params=pltpu.CompilerParams(vmem_limit_bytes=WHOLE),
+        cost_estimate=pl.CostEstimate(
+            flops=0, bytes_accessed=2 * sum(a.nbytes for a in arrays), transcendentals=0
+        ),
+    )(*(pltpu.with_memory_space_constraint(a, pltpu.HBM) for a in arrays))
 
 
 def tile_call(tiles, halo, own):
@@ -253,50 +282,31 @@
     )(tiles, halo, *own)
 
 
-def score_call(first, clips, order, spectrum, inverse_rms, consts, count, before):
+def score_call(first, clips, order, spectrum, inverse_rms, consts, blocks, per_block):
     n = len(clips)
-    layers, e, _ = clips[0].shape
     rows, columns = inverse_rms.shape
     args = (*clips, order, spectrum, inverse_rms, *consts)
-    in_specs = [INSIDE] * len(args)
-    aliases = {}
-    if before is not None:
-        in_specs.append(OUTSIDE)
-        aliases = {len(args): 0}
-        args += (before,)
 
     def kernel(*refs):
-        scores, peaks, result, sems = refs[-4:]
+        scores, peaks = refs[-2:]
         order, *rest = refs[n : n + 7]
-        own = lax.axis_index("groups") % 2 * 2 + lax.axis_index("tile") % 2
-        slots = [own ^ (first + i) for i in range(n)]
+        own = lax.axis_index("groups") % blocks * per_block + lax.axis_index("tile") % per_block
         row = lax.broadcasted_iota(jnp.int32, peaks.shape, 0)
+        column = lax.broadcasted_iota(jnp.int32, peaks.shape, 1)
         best = jnp.full(peaks.shape, -jnp.inf, jnp.float32)
-        copies = []
         for i in range(n):
-            if i > 1:
-                copies[i - 2].wait()
-            largest = score_clip(order, refs[i], *rest, result.at[i % 2])
-            best = jnp.where(row == slots[i], largest, best)
-            copies.append(pltpu.make_async_copy(result.at[i % 2], scores.at[slots[i]], sems.at[i % 2]))
-            copies[i].start()
+            largest = score_clip(order, refs[i], *rest, scores.at[i])
+            best = jnp.where(row * per_block + column == own ^ (first + i), largest, best)
         peaks[...] = best
-        for copy in copies[-2:]:
-            copy.wait()
 
     return pl.pallas_call(
         kernel,
-        in_specs=in_specs,
-        out_specs=(OUTSIDE, INSIDE),
+        in_specs=[INSIDE] * len(args),
+        out_specs=(INSIDE, INSIDE),
         out_shape=(
-            jax.ShapeDtypeStruct((count, rows, columns), jnp.float32),
-            jax.ShapeDtypeStruct((8, 128), jnp.float32),
+            pltpu.VMEM((n, rows, columns), jnp.float32),
+            pltpu.VMEM((blocks, per_block), jnp.float32),
         ),
-        scratch_shapes=[
-            pltpu.VMEM((2, rows, columns), jnp.float32),
-            pltpu.SemaphoreType.DMA((2,)),
-        ],
-        input_output_aliases=aliases,
         compiler_params=pltpu.CompilerParams(vmem_limit_bytes=VMEM),
         cost_estimate=pl.CostEstimate(
             flops=n * 1_300_000_000, bytes_accessed=6_000_000, transcendentals=0
@@ -304,16 +314,37 @@
     )(*args)
 
 
+def write_call(results, blocks, per_block):
+    count = blocks * per_block
+    rows, columns = results[0].shape[1:]
+
+    def kernel(*refs):
+        scores, sems = refs[-2:]
+        own = lax.axis_index("groups") % blocks * per_block + lax.axis_index("tile") % per_block
+        copies = []
+        for ref in refs[:-2]:
+            for i in range(ref.shape[0]):
+                k = len(copies)
+                copies.append(pltpu.make_async_copy(ref.at[i], scores.at[own ^ k], sems.at[k]))
+                copies[k].start()
+        for copy in copies:
+            copy.wait()
+
+    return pl.pallas_call(
+        kernel,
+        in_specs=[INSIDE] * len(results),
+        out_specs=OUTSIDE,
+        out_shape=jax.ShapeDtypeStruct((count, rows, columns), jnp.float32),
+        scratch_shapes=[pltpu.SemaphoreType.DMA((count,))],
+        compiler_params=pltpu.CompilerParams(vmem_limit_bytes=WHOLE),
+        cost_estimate=pl.CostEstimate(
+            flops=0, bytes_accessed=2 * count * rows * columns * 4, transcendentals=0
+        ),
+    )(*results)
+
+
 def swap(block, axis, distance):
     return lax.ppermute(block, axis, [(i, i ^ distance) for i in range(lax.axis_size(axis))])
-
-
-def cross_swap(block):
-    groups, devices = lax.axis_size("groups"), lax.axis_size("tile")
-    route = [
-        (g * devices + i, (g ^ 1) * devices + (i ^ 1)) for g in range(groups) for i in range(devices)
-    ]
-    return lax.ppermute(block, ("groups", "tile"), route)
 
 
 def local(tiles, library, block_owner, block_clips, layer_order):
@@ -330,14 +361,15 @@
     mine, theirs, edge, differ, order = pick_call(
         block_owner, block_clips, layer_order, library, tiles, bits
     )
-    own = (band_rows, band_cols, tile_right, tile_left)
-    edge, tiles, own = lax.optimization_barrier((edge, tiles, own))
     halo = lax.ppermute(edge, "tile", [(i, i - 1) for i in range(1, devices)])
 
     def take(k, own, got):
         return jnp.where(differ[k][None, None, :] == 0, own, got)
 
     held = take(0, mine, swap(theirs, "tile", 1))
+    own = (tiles, band_rows, band_cols, tile_right, tile_left)
+    held, own = lax.optimization_barrier((held, own))
+    tiles, *own = hold_call(own)
     consts = (clip_left, clip_right, back_left, back_right)
     for k in range(1, bits):
         got = swap(held, "tile", 1 << k)
@@ -349,20 +381,24 @@
             held, spectrum, inverse_rms = lax.optimization_barrier((held, spectrum, inverse_rms))
     twin = swap(held, "tile", 1)
     other = swap(held, "groups", 1)
-    cross = cross_swap(held)
-    count = blocks * per_block
-    shared = (order, spectrum, inverse_rms, consts, count)
-    scores, best = score_call(0, (held, twin), *shared, None)
-    scores, more = score_call(2, (other, cross), *shared, scores)
+    shared = (order, spectrum, inverse_rms, consts, blocks, per_block)
+    near, best = score_call(0, (held, twin), *shared)
+    other, near = lax.optimization_barrier((other, near))
+    cross = swap(other, "tile", 1)
+    far, more = score_call(2, (other,), *shared)
     best = jnp.maximum(best, more)
-    distance = 1
-    while distance < devices:
-        best = jnp.maximum(best, swap(best, "tile", distance))
-        distance *= 2
-    return (
-        scores.reshape(blocks, per_block, rows, columns),
-        best[:count, 0].reshape(blocks, per_block),
-    )
+    cross, far = lax.optimization_barrier((cross, far))
+    last, more = score_call(3, (cross,), *shared)
+    best = jnp.maximum(best, more)
+    best = jnp.maximum(best, swap(best, "tile", 1))
+    best, near, far, last = lax.optimization_barrier((best, near, far, last))
+    scores = write_call((near, far, last), blocks, per_block)
+    for k in range(1, bits):
+        got = swap(best, "tile", 1 << k)
+        if k == 2:
+            got, scores = lax.optimization_barrier((got, scores))
+        best = jnp.maximum(best, got)
+    return scores.reshape(blocks, per_block, rows, columns), best
 
 
 def solution(mesh):

time: 55.8 us -> 50 us (0.90)
  waiting for transfers between devices: 19.2 us -> 15.3 us
  other arithmetic: 1.82 us -> 0.65 us
  local copies, waits for them, and re-layouts: 0.83 us -> 0.01 us
    ppermute x10 -> x11, waiting for transfers between devices: 19.2 us -> 15.3 us  [swap(): lax.ppermute(block, axis, [(i, i ^ distance) for i in range(lax.axis_size...]
    pallas_call x2 -> x5, Pallas kernels: 10.3 us -> 12 us  [the longest x3 8.74 us: score_call(): pl.pallas_call(kernel, in_specs=[INSIDE] * len(args), out_specs=(INSIDE,...]
    ppermute x1 -> x0, starting transfers between devices: 1.61 us -> none  [cross_swap(): return lax.ppermute(block, ('groups', 'tile'), route)]
    ppermute x10 -> x11, starting transfers between devices: 13.5 us -> 14.8 us  [swap(): lax.ppermute(block, axis, [(i, i ^ distance) for i in range(lax.axis_size...]
    pallas_call x1, Pallas kernels: 3 us -> 1.77 us  [pick_call(): pl.pallas_call(kernel, out_shape=(clip, clip, edge, table, table), in_spe...]
    select_n x4, other arithmetic: 0.97 us -> 0.07 us  [take(): return jnp.where(differ[k][None, None, :] == 0, own, got)]
    eq x1, other arithmetic: 0.84 us -> 0.01 us  [take(): return jnp.where(differ[k][None, None, :] == 0, own, got)]
    another operation x1 -> x0, local copies, waits for them, and re-layouts: 0.65 us -> none  [local(): best[:count, 0].reshape(blocks, per_block)]
  transfers between devices with their start and end apart: 12 -> 12, of which waited for: 9 -> 9; matrix products, arithmetic and copies ran while one was open for 2% -> 0% of each run, Pallas kernels for 15% -> 26%
where the time goes in v2:
time: 50 us; the launch traced here: 49.8 us
  Pallas kernels  17 us (34%)
  starting transfers between devices  16.1 us (32%)
  waiting for transfers between devices  15.3 us (31%)
  between operations  0.77 us (2%)
  other arithmetic  0.65 us (1%)
    ppermute x11, waiting for transfers between devices, swap(): lax.ppermute(block, axis, [(i, i ^ distance) for i in range(lax.axis_size...  15.3 us
    ppermute x11, starting transfers between devices, swap(): lax.ppermute(block, axis, [(i, i ^ distance) for i in range(lax.axis_size...  14.8 us
    pallas_call x3, Pallas kernels, score_call(): pl.pallas_call(kernel, in_specs=[INSIDE] * len(args), out_specs=(INSIDE,...  8.74 us
    pallas_call x1, Pallas kernels, tile_call(): pl.pallas_call(tile_kernel, in_specs=[INSIDE] * (2 + len(own)), out_specs...  3.2 us
    pallas_call x1, Pallas kernels, hold_call(): pl.pallas_call(kernel, out_shape=tuple((pltpu.VMEM(a.shape, a.dtype) for...  1.85 us
    pallas_call x1, Pallas kernels, pick_call(): pl.pallas_call(kernel, out_shape=(clip, clip, edge, table, table), in_spe...  1.77 us
    pallas_call x1, Pallas kernels, write_call(): pl.pallas_call(kernel, in_specs=[INSIDE] * len(results), out_specs=OUTSID...  1.43 us
    ppermute x1, starting transfers between devices, local(): halo = lax.ppermute(edge, 'tile', [(i, i - 1) for i in range(1, devices)])  1.28 us
  transfers between devices with their start and end apart: 12, of which 9 were waited for; matrix products, arithmetic and copies ran while one was open for 0% of the time, Pallas kernels for 26%

profile of v2, /device:TPU:0, one launch (start us, length us, event | category | flops | bytes accessed | tf_op | source)
XLA Modules:
  0.0 49.8 jit_solution(15742458153417418485)
XLA Ops:
  0.6 1.8 %shard_map.140 = (f32[2,128,128]{2,1,0:T(8,128)S(1)}, f32[2,128,128]{2,1,0:T(8,128)S(1)}, f32[2,128,384]{2,1,0:T(8,128)S(1)}, s32[8,128]{1,0:T(8,128)S(1)}, s32[8,128]{1,0:T(8,128)S(1)}) custom-call(s32[2]{0:T(128)} %owner_in.1, s32[2,2]{1,0:T(2,128)} %clips_in.1, s32[1,2]{1,0:T(1,128)} %order_in.1, f32[8,2,128,128]{3,2,1,0:T(8,128)} %library.1, ...), custom_call_target="tpu_custom_call" | custom-call | tf_op jit(solution)/shard_map/pallas_call | solution.py:229
  2.4 0.5 %collective-permute-start = (f32[2,128,128]{2,1,0:T(8,128)S(1)}, f32[2,128,128]{2,1,0:T(8,128)S(1)}, u32[]{:S(2)}, u32[]{:S(2)}) collective-permute-start(f32[2,128,128]{2,1,0:T(8,128)S(1)} %get-tuple-element.43), channel_id=1, source_target_pairs={{0,1},{1,0},{2,3},{3,2},{4,5},{5,4},{6,7},{7,6},{8,9},{9,8},{10,11... | collective-permute-start | bytes 393224 | tf_op jit(solution)/shard_map/ppermute | solution.py:347
  2.9 1.0 %collective-permute-done = f32[2,128,128]{2,1,0:T(8,128)S(1)} collective-permute-done((f32[2,128,128]{2,1,0:T(8,128)S(1)}, f32[2,128,128]{2,1,0:T(8,128)S(1)}, u32[]{:S(2)}, u32[]{:S(2)}) %collective-permute-start) | collective-permute-done | bytes 131104 | tf_op jit(solution)/shard_map/ppermute | solution.py:347
  3.9 2.9 %collective-permute-start.1 = (f32[2,128,128]{2,1,0:T(8,128)S(1)}, f32[2,128,128]{2,1,0:T(8,128)S(1)}, u32[]{:S(2)}, u32[]{:S(2)}) collective-permute-start(f32[2,128,128]{2,1,0:T(8,128)S(1)} %broadcast_select_fusion), channel_id=1, source_target_pairs={{0,2},{1,3},{2,0},{3,1},{4,6},{5,7},{6,4},{7,5},{8,10},{9,11},{10,... | collective-permute-start | bytes 393224 | tf_op jit(solution)/shard_map/ppermute | solution.py:347
  6.9 1.3 %collective-permute-start.3 = (f32[2,128,384]{2,1,0:T(8,128)S(1)}, f32[2,128,384]{2,1,0:T(8,128)S(1)}, u32[]{:S(2)}, u32[]{:S(2)}) collective-permute-start(f32[2,128,384]{2,1,0:T(8,128)S(1)} %get-tuple-element.45), channel_id=1, source_target_pairs={{1,0},{2,1},{3,2},{4,3},{5,4},{6,5},{7,6},{8,7},{9,8},{10,9},{11,1... | collective-permute-start | bytes 1179656 | tf_op jit(solution)/shard_map/ppermute | solution.py:364
  8.2 2.5 %collective-permute-done.1 = f32[2,128,128]{2,1,0:T(8,128)S(1)} collective-permute-done((f32[2,128,128]{2,1,0:T(8,128)S(1)}, f32[2,128,128]{2,1,0:T(8,128)S(1)}, u32[]{:S(2)}, u32[]{:S(2)}) %collective-permute-start.1) | collective-permute-done | bytes 131104 | tf_op jit(solution)/shard_map/ppermute | solution.py:347
  10.7 1.9 %collective-permute-start.2 = (f32[2,128,128]{2,1,0:T(8,128)S(1)}, f32[2,128,128]{2,1,0:T(8,128)S(1)}, u32[]{:S(2)}, u32[]{:S(2)}) collective-permute-start(f32[2,128,128]{2,1,0:T(8,128)S(1)} %broadcast_select_fusion.1), channel_id=1, source_target_pairs={{0,4},{1,5},{2,6},{3,7},{4,0},{5,1},{6,2},{7,3},{8,12},{9,13},{10,... | collective-permute-start | bytes 393224 | tf_op jit(solution)/shard_map/ppermute | solution.py:347
  12.6 1.8 %shard_map.141 = (f32[2,384,384]{2,1,0:T(8,128)S(1)}, bf16[128,512]{1,0:T(8,128)(2,1)S(1)}, bf16[512,128]{1,0:T(8,128)(2,1)S(1)}, bf16[2,768,256]{2,1,0:T(8,128)(2,1)S(1)}, bf16[2,256,768]{2,1,0:T(8,128)(2,1)S(1)}) custom-call(f32[2,384,384]{2,1,0:T(8,128)} %refs_0_, bf16[128,512]{1,0:T(8,128)(2,1)} %constant.24.clone.refs_1_, ...), custom_call_target="tpu_custom_call" | custom-call | bytes 6029312 | tf_op jit(solution)/shard_map/pallas_call | solution.py:256
  14.4 4.5 %collective-permute-done.2 = f32[2,128,128]{2,1,0:T(8,128)S(1)} collective-permute-done((f32[2,128,128]{2,1,0:T(8,128)S(1)}, f32[2,128,128]{2,1,0:T(8,128)S(1)}, u32[]{:S(2)}, u32[]{:S(2)}) %collective-permute-start.2) | collective-permute-done | bytes 131104 | tf_op jit(solution)/shard_map/ppermute | solution.py:347
  18.9 0.0 collective-permute-done.3.halo
  18.9 2.9 %collective-permute-start.4 = (f32[2,128,128]{2,1,0:T(8,128)S(1)}, f32[2,128,128]{2,1,0:T(8,128)S(1)}, u32[]{:S(2)}, u32[]{:S(2)}) collective-permute-start(f32[2,128,128]{2,1,0:T(8,128)S(1)} %broadcast_select_fusion.2), channel_id=1, source_target_pairs={{0,8},{1,9},{2,10},{3,11},{4,12},{5,13},{6,14},{7,15},{8,0},{9,1},... | collective-permute-start | bytes 393224 | tf_op jit(solution)/shard_map/ppermute | solution.py:347
  21.8 0.0 copy-start
  21.8 0.0 copy-start.1
  21.8 0.0 copy-start.2
  21.8 0.0 copy-start.3
  21.8 3.2 %shard_map.142 = (f32[2,4,256,256]{3,2,1,0:T(8,128)S(1)}, f32[384,384]{1,0:T(8,128)S(1)}) custom-call(f32[2,384,384]{2,1,0:T(8,128)S(1)} %get-tuple-element.52.tile, f32[2,128,384]{2,1,0:T(8,128)S(1)} %collective-permute-done.3.halo, bf16[128,512]{1,0:T(8,128)(2,1)S(1)} %get-tuple-element.54.band_rows, bf16[512,128]{1,0:T(8,128)(2,1)S(1)} %get-tuple-element.55.band_cols, ...), custom_call_target="tpu_custom_call" | custom-call | flops 2000000000 | bytes 6000000 | tf_op jit(solution)/shard_map/pallas_call | solution.py:272
  25.0 0.2 collective-permute-done.4
  25.3 0.1 collective-permute-start.5
  25.3 1.6 %collective-permute-start.6 = (f32[2,128,128]{2,1,0:T(8,128)S(1)}, f32[2,128,128]{2,1,0:T(8,128)S(1)}, u32[]{:S(2)}, u32[]{:S(2)}) collective-permute-start(f32[2,128,128]{2,1,0:T(8,128)S(1)} %broadcast_select_fusion.3.refs_0_), channel_id=1, source_target_pairs={{0,16},{16,0},{1,17},{17,1},{2,18},{18,2},{3,19},{19,3},{4,20},{20... | collective-permute-start | bytes 393224 | tf_op jit(solution)/shard_map/ppermute | solution.py:347
  26.9 0.0 collective-permute-done.5.refs_1_
  26.9 0.0 copy-done
  26.9 0.0 copy-done.1
  26.9 0.0 copy-done.2
  26.9 0.0 copy-done.3
  26.9 4.1 %shard_map.143 = (f32[2,384,384]{2,1,0:T(8,128)S(1)}, f32[2,2]{1,0:T(2,128)S(1)}) custom-call(f32[2,128,128]{2,1,0:T(8,128)S(1)} %broadcast_select_fusion.3.refs_0_, f32[2,128,128]{2,1,0:T(8,128)S(1)} %collective-permute-done.5.refs_1_, s32[8,128]{1,0:T(8,128)S(1)} %get-tuple-element.61.refs_2_.refs_1_, ...), custom_call_target="tpu_custom_call" | custom-call | flops 2600000000 | bytes 6000000 | tf_op jit(solution)/shard_map/pallas_call | solution.py:302
  31.1 0.2 collective-permute-done.6.refs_0_
  31.3 0.1 collective-permute-start.7
  31.3 2.3 %shard_map.144 = (f32[1,384,384]{2,1,0:T(8,128)S(1)}, f32[2,2]{1,0:T(2,128)S(1)}) custom-call(f32[2,128,128]{2,1,0:T(8,128)S(1)} %collective-permute-done.6.refs_0_, s32[8,128]{1,0:T(8,128)S(1)} %get-tuple-element.61.refs_2_.refs_1_, f32[2,4,256,256]{3,2,1,0:T(8,128)S(1)} %get-tuple-element.62.refs_3_.refs_2_, ...), custom_call_target="tpu_custom_call" | custom-call | flops 1300000000 | bytes 6000000 | tf_op jit(solution)/shard_map/pallas_call | solution.py:302
  33.6 0.0 collective-permute-done.7.refs_0_
  33.6 2.3 %shard_map.145 = (f32[1,384,384]{2,1,0:T(8,128)S(1)}, f32[2,2]{1,0:T(2,128)S(1)}) custom-call(f32[2,128,128]{2,1,0:T(8,128)S(1)} %collective-permute-done.7.refs_0_, s32[8,128]{1,0:T(8,128)S(1)} %get-tuple-element.61.refs_2_.refs_1_, f32[2,4,256,256]{3,2,1,0:T(8,128)S(1)} %get-tuple-element.62.refs_3_.refs_2_, ...), custom_call_target="tpu_custom_call" | custom-call | flops 1300000000 | bytes 6000000 | tf_op jit(solution)/shard_map/pallas_call | solution.py:302
  36.0 0.5 %collective-permute-start.8 = (f32[2,2]{1,0:T(2,128)S(1)}, f32[2,2]{1,0:T(2,128)S(1)}, u32[]{:S(2)}, u32[]{:S(2)}) collective-permute-start(f32[2,2]{1,0:T(2,128)S(1)} %maximum_maximum_fusion), channel_id=1, source_target_pairs={{0,1},{1,0},{2,3},{3,2},{4,5},{5,4},{6,7},{7,6},{8,9},{9,8},{10,11... | collective-permute-start | bytes 56 | tf_op jit(solution)/shard_map/ppermute | solution.py:347
  36.5 0.8 %collective-permute-done.8 = f32[2,2]{1,0:T(2,128)S(1)} collective-permute-done((f32[2,2]{1,0:T(2,128)S(1)}, f32[2,2]{1,0:T(2,128)S(1)}, u32[]{:S(2)}, u32[]{:S(2)}) %collective-permute-start.8) | collective-permute-done | bytes 48 | tf_op jit(solution)/shard_map/ppermute | solution.py:347
  37.3 2.3 %collective-permute-start.9 = (f32[2,2]{1,0:T(2,128)S(1)}, f32[2,2]{1,0:T(2,128)S(1)}, u32[]{:S(2)}, u32[]{:S(2)}) collective-permute-start(f32[2,2]{1,0:T(2,128)S(1)} %max.20), channel_id=1, source_target_pairs={{0,2},{1,3},{2,0},{3,1},{4,6},{5,7},{6,4},{7,5},{8,10},{9,11},{10,... | collective-permute-start | bytes 56 | tf_op jit(solution)/shard_map/ppermute | solution.py:347
  39.6 1.4 %shard_map.146 = f32[4,384,384]{2,1,0:T(8,128)} custom-call(f32[2,384,384]{2,1,0:T(8,128)S(1)} %get-tuple-element.75.refs_0_, f32[1,384,384]{2,1,0:T(8,128)S(1)} %get-tuple-element.76.refs_1_, f32[1,384,384]{2,1,0:T(8,128)S(1)} %get-tuple-element.77.refs_2_), custom_call_target="tpu_custom_call" | custom-call | bytes 4718592 | tf_op jit(solution)/shard_map/pallas_call | solution.py:333
  41.0 0.1 collective-permute-done.9
  41.2 0.0 collective-permute-start.10
  41.2 3.6 %collective-permute-done.10 = f32[2,2]{1,0:T(2,128)S(1)} collective-permute-done((f32[2,2]{1,0:T(2,128)S(1)}, f32[2,2]{1,0:T(2,128)S(1)}, u32[]{:S(2)}, u32[]{:S(2)}) %collective-permute-start.10) | collective-permute-done | bytes 48 | tf_op jit(solution)/shard_map/ppermute | solution.py:347
  44.7 2.1 %collective-permute-start.11 = (f32[2,2]{1,0:T(2,128)S(1)}, f32[2,2]{1,0:T(2,128)S(1)}, u32[]{:S(2)}, u32[]{:S(2)}) collective-permute-start(f32[2,2]{1,0:T(2,128)S(1)} %max.22), channel_id=1, source_target_pairs={{0,8},{1,9},{2,10},{3,11},{4,12},{5,13},{6,14},{7,15},{8,0},{9,1},... | collective-permute-start | bytes 56 | tf_op jit(solution)/shard_map/ppermute | solution.py:347
  46.9 2.3 %collective-permute-done.11 = f32[2,2]{1,0:T(2,128)S(1)} collective-permute-done((f32[2,2]{1,0:T(2,128)S(1)}, f32[2,2]{1,0:T(2,128)S(1)}, u32[]{:S(2)}, u32[]{:S(2)}) %collective-permute-start.11) | collective-permute-done | bytes 48 | tf_op jit(solution)/shard_map/ppermute | solution.py:347
  49.2 0.6 %max.23 = f32[2,2]{1,0:T(2,128)} maximum(f32[2,2]{1,0:T(2,128)S(1)} %max.22, f32[2,2]{1,0:T(2,128)S(1)} %collective-permute-done.11) | non-fusion elementwise | flops 4 | bytes 48 | tf_op jit(solution)/shard_map/max | solution.py:400
  (9 shorter events, 0.1 us)
Async XLA Ops:
  2.4 1.5 %collective-permute-start = (f32[2,128,128]{2,1,0:T(8,128)S(1)}, f32[2,128,128]{2,1,0:T(8,128)S(1)}, u32[]{:S(2)}, u32[]{:S(2)}) collective-permute-start(f32[2,128,128]{2,1,0:T(8,128)S(1)} %get-tuple-element.43), channel_id=1, source_target_pairs={{0,1},{1,0},{2,3},{3,2},{4,5},{5,4},{6,7},{7,6},{8,9},{9,8},{10,11... | collective-permute-start | bytes 393224 | tf_op jit(solution)/shard_map/ppermute | solution.py:347
  3.9 6.8 %collective-permute-start.1 = (f32[2,128,128]{2,1,0:T(8,128)S(1)}, f32[2,128,128]{2,1,0:T(8,128)S(1)}, u32[]{:S(2)}, u32[]{:S(2)}) collective-permute-start(f32[2,128,128]{2,1,0:T(8,128)S(1)} %broadcast_select_fusion), channel_id=1, source_target_pairs={{0,2},{1,3},{2,0},{3,1},{4,6},{5,7},{6,4},{7,5},{8,10},{9,11},{10,... | collective-permute-start | bytes 393224 | tf_op jit(solution)/shard_map/ppermute | solution.py:347
  6.9 12.0 %collective-permute-start.3 = (f32[2,128,384]{2,1,0:T(8,128)S(1)}, f32[2,128,384]{2,1,0:T(8,128)S(1)}, u32[]{:S(2)}, u32[]{:S(2)}) collective-permute-start(f32[2,128,384]{2,1,0:T(8,128)S(1)} %get-tuple-element.45), channel_id=1, source_target_pairs={{1,0},{2,1},{3,2},{4,3},{5,4},{6,5},{7,6},{8,7},{9,8},{10,9},{11,1... | collective-permute-start | bytes 1179656 | tf_op jit(solution)/shard_map/ppermute | solution.py:364
  10.7 8.2 %collective-permute-start.2 = (f32[2,128,128]{2,1,0:T(8,128)S(1)}, f32[2,128,128]{2,1,0:T(8,128)S(1)}, u32[]{:S(2)}, u32[]{:S(2)}) collective-permute-start(f32[2,128,128]{2,1,0:T(8,128)S(1)} %broadcast_select_fusion.1), channel_id=1, source_target_pairs={{0,4},{1,5},{2,6},{3,7},{4,0},{5,1},{6,2},{7,3},{8,12},{9,13},{10,... | collective-permute-start | bytes 393224 | tf_op jit(solution)/shard_map/ppermute | solution.py:347
  18.9 6.3 %collective-permute-start.4 = (f32[2,128,128]{2,1,0:T(8,128)S(1)}, f32[2,128,128]{2,1,0:T(8,128)S(1)}, u32[]{:S(2)}, u32[]{:S(2)}) collective-permute-start(f32[2,128,128]{2,1,0:T(8,128)S(1)} %broadcast_select_fusion.2), channel_id=1, source_target_pairs={{0,8},{1,9},{2,10},{3,11},{4,12},{5,13},{6,14},{7,15},{8,0},{9,1},... | collective-permute-start | bytes 393224 | tf_op jit(solution)/shard_map/ppermute | solution.py:347
  21.8 5.1 %copy-start = (bf16[2,768,256]{2,1,0:T(8,128)(2,1)S(1)}, bf16[2,768,256]{2,1,0:T(8,128)(2,1)}, u32[]{:S(2)}) copy-start(bf16[2,768,256]{2,1,0:T(8,128)(2,1)} %constant.23.clone.refs_8_.refs_7_) | copy-start | bytes 2359300
  21.8 5.1 %copy-start.1 = (bf16[2,256,768]{2,1,0:T(8,128)(2,1)S(1)}, bf16[2,256,768]{2,1,0:T(8,128)(2,1)}, u32[]{:S(2)}) copy-start(bf16[2,256,768]{2,1,0:T(8,128)(2,1)} %constant.22.clone.refs_7_.refs_6_) | copy-start | bytes 2359300
  21.8 5.1 %copy-start.2 = (bf16[384,512]{1,0:T(8,128)(2,1)S(1)}, bf16[384,512]{1,0:T(8,128)(2,1)}, u32[]{:S(2)}) copy-start(bf16[384,512]{1,0:T(8,128)(2,1)} %constant.21.clone.refs_6_.refs_5_) | copy-start | bytes 1179652
  21.8 5.1 %copy-start.3 = (bf16[512,384]{1,0:T(8,128)(2,1)S(1)}, bf16[512,384]{1,0:T(8,128)(2,1)}, u32[]{:S(2)}) copy-start(bf16[512,384]{1,0:T(8,128)(2,1)} %constant.20.clone.refs_5_.refs_4_) | copy-start | bytes 1179652
  25.3 1.6 %collective-permute-start.5 = (f32[2,128,128]{2,1,0:T(8,128)S(1)}, f32[2,128,128]{2,1,0:T(8,128)S(1)}, u32[]{:S(2)}, u32[]{:S(2)}) collective-permute-start(f32[2,128,128]{2,1,0:T(8,128)S(1)} %broadcast_select_fusion.3.refs_0_), channel_id=1, source_target_pairs={{0,1},{1,0},{2,3},{3,2},{4,5},{5,4},{6,7},{7,6},{8,9},{9,8},{10,11... | collective-permute-start | bytes 393224 | tf_op jit(solution)/shard_map/ppermute | solution.py:347
  25.3 5.9 %collective-permute-start.6 = (f32[2,128,128]{2,1,0:T(8,128)S(1)}, f32[2,128,128]{2,1,0:T(8,128)S(1)}, u32[]{:S(2)}, u32[]{:S(2)}) collective-permute-start(f32[2,128,128]{2,1,0:T(8,128)S(1)} %broadcast_select_fusion.3.refs_0_), channel_id=1, source_target_pairs={{0,16},{16,0},{1,17},{17,1},{2,18},{18,2},{3,19},{19,3},{4,20},{20... | collective-permute-start | bytes 393224 | tf_op jit(solution)/shard_map/ppermute | solution.py:347
  31.3 2.4 %collective-permute-start.7 = (f32[2,128,128]{2,1,0:T(8,128)S(1)}, f32[2,128,128]{2,1,0:T(8,128)S(1)}, u32[]{:S(2)}, u32[]{:S(2)}) collective-permute-start(f32[2,128,128]{2,1,0:T(8,128)S(1)} %collective-permute-done.6.refs_0_), channel_id=1, source_target_pairs={{0,1},{1,0},{2,3},{3,2},{4,5},{5,4},{6,7},{7,6},{8,9},{9,8},{10,11... | collective-permute-start | bytes 393224 | tf_op jit(solution)/shard_map/ppermute | solution.py:347
  36.0 1.3 %collective-permute-start.8 = (f32[2,2]{1,0:T(2,128)S(1)}, f32[2,2]{1,0:T(2,128)S(1)}, u32[]{:S(2)}, u32[]{:S(2)}) collective-permute-start(f32[2,2]{1,0:T(2,128)S(1)} %maximum_maximum_fusion), channel_id=1, source_target_pairs={{0,1},{1,0},{2,3},{3,2},{4,5},{5,4},{6,7},{7,6},{8,9},{9,8},{10,11... | collective-permute-start | bytes 56 | tf_op jit(solution)/shard_map/ppermute | solution.py:347
  37.3 3.8 %collective-permute-start.9 = (f32[2,2]{1,0:T(2,128)S(1)}, f32[2,2]{1,0:T(2,128)S(1)}, u32[]{:S(2)}, u32[]{:S(2)}) collective-permute-start(f32[2,2]{1,0:T(2,128)S(1)} %max.20), channel_id=1, source_target_pairs={{0,2},{1,3},{2,0},{3,1},{4,6},{5,7},{6,4},{7,5},{8,10},{9,11},{10,... | collective-permute-start | bytes 56 | tf_op jit(solution)/shard_map/ppermute | solution.py:347
  41.2 3.6 %collective-permute-start.10 = (f32[2,2]{1,0:T(2,128)S(1)}, f32[2,2]{1,0:T(2,128)S(1)}, u32[]{:S(2)}, u32[]{:S(2)}) collective-permute-start(f32[2,2]{1,0:T(2,128)S(1)} %max.21), channel_id=1, source_target_pairs={{0,4},{1,5},{2,6},{3,7},{4,0},{5,1},{6,2},{7,3},{8,12},{9,13},{10,... | collective-permute-start | bytes 56 | tf_op jit(solution)/shard_map/ppermute | solution.py:347
  44.7 4.5 %collective-permute-start.11 = (f32[2,2]{1,0:T(2,128)S(1)}, f32[2,2]{1,0:T(2,128)S(1)}, u32[]{:S(2)}, u32[]{:S(2)}) collective-permute-start(f32[2,2]{1,0:T(2,128)S(1)} %max.22), channel_id=1, source_target_pairs={{0,8},{1,9},{2,10},{3,11},{4,12},{5,13},{6,14},{7,15},{8,0},{9,1},... | collective-permute-start | bytes 56 | tf_op jit(solution)/shard_map/ppermute | solution.py:347

commit v3 on v2

--- a/solution.py
+++ b/solution.py
@@ -390,12 +390,13 @@
     cross, far = lax.optimization_barrier((cross, far))
     last, more = score_call(3, (cross,), *shared)
     best = jnp.maximum(best, more)
-    best = jnp.maximum(best, swap(best, "tile", 1))
+    tail = [*range(1, bits), 0]
+    best = jnp.maximum(best, swap(best, "tile", 1 << tail[0]))
     best, near, far, last = lax.optimization_barrier((best, near, far, last))
     scores = write_call((near, far, last), blocks, per_block)
-    for k in range(1, bits):
+    for step, k in enumerate(tail[1:], 1):
         got = swap(best, "tile", 1 << k)
-        if k == 2:
+        if step == 2:
             got, scores = lax.optimization_barrier((got, scores))
         best = jnp.maximum(best, got)
     return scores.reshape(blocks, per_block, rows, columns), best

time: 50 us -> 49.8 us (level)
  starting transfers between devices: 16.1 us -> 15.6 us
where the time goes in v3:
time: 49.8 us; the launch traced here: 49.6 us
  Pallas kernels  17 us (34%)
  starting transfers between devices  15.6 us (31%)
  waiting for transfers between devices  15.6 us (31%)
  between operations  0.77 us (2%)
  other arithmetic  0.65 us (1%)
    ppermute x11, waiting for transfers between devices, swap(): lax.ppermute(block, axis, [(i, i ^ distance) for i in range(lax.axis_size...  15.6 us
    ppermute x11, starting transfers between devices, swap(): lax.ppermute(block, axis, [(i, i ^ distance) for i in range(lax.axis_size...  14.3 us
    pallas_call x3, Pallas kernels, score_call(): pl.pallas_call(kernel, in_specs=[INSIDE] * len(args), out_specs=(INSIDE,...  8.74 us
    pallas_call x1, Pallas kernels, tile_call(): pl.pallas_call(tile_kernel, in_specs=[INSIDE] * (2 + len(own)), out_specs...  3.2 us
    pallas_call x1, Pallas kernels, hold_call(): pl.pallas_call(kernel, out_shape=tuple((pltpu.VMEM(a.shape, a.dtype) for...  1.85 us
    pallas_call x1, Pallas kernels, pick_call(): pl.pallas_call(kernel, out_shape=(clip, clip, edge, table, table), in_spe...  1.78 us
    pallas_call x1, Pallas kernels, write_call(): pl.pallas_call(kernel, in_specs=[INSIDE] * len(results), out_specs=OUTSID...  1.43 us
    ppermute x1, starting transfers between devices, local(): halo = lax.ppermute(edge, 'tile', [(i, i - 1) for i in range(1, devices)])  1.28 us
  transfers between devices with their start and end apart: 12, of which 9 were waited for; matrix products, arithmetic and copies ran while one was open for 0% of the time, Pallas kernels for 26%

profile of v3, /device:TPU:0, one launch (start us, length us, event | category | flops | bytes accessed | tf_op | source)
XLA Modules:
  0.0 49.6 jit_solution(13575120229759361658)
XLA Ops:
  0.6 1.8 %shard_map.140 = (f32[2,128,128]{2,1,0:T(8,128)S(1)}, f32[2,128,128]{2,1,0:T(8,128)S(1)}, f32[2,128,384]{2,1,0:T(8,128)S(1)}, s32[8,128]{1,0:T(8,128)S(1)}, s32[8,128]{1,0:T(8,128)S(1)}) custom-call(s32[2]{0:T(128)} %owner_in.1, s32[2,2]{1,0:T(2,128)} %clips_in.1, s32[1,2]{1,0:T(1,128)} %order_in.1, f32[8,2,128,128]{3,2,1,0:T(8,128)} %library.1, ...), custom_call_target="tpu_custom_call" | custom-call | tf_op jit(solution)/shard_map/pallas_call | solution.py:229
  2.4 0.5 %collective-permute-start = (f32[2,128,128]{2,1,0:T(8,128)S(1)}, f32[2,128,128]{2,1,0:T(8,128)S(1)}, u32[]{:S(2)}, u32[]{:S(2)}) collective-permute-start(f32[2,128,128]{2,1,0:T(8,128)S(1)} %get-tuple-element.43), channel_id=1, source_target_pairs={{0,1},{1,0},{2,3},{3,2},{4,5},{5,4},{6,7},{7,6},{8,9},{9,8},{10,11... | collective-permute-start | bytes 393224 | tf_op jit(solution)/shard_map/ppermute | solution.py:347
  2.9 1.0 %collective-permute-done = f32[2,128,128]{2,1,0:T(8,128)S(1)} collective-permute-done((f32[2,128,128]{2,1,0:T(8,128)S(1)}, f32[2,128,128]{2,1,0:T(8,128)S(1)}, u32[]{:S(2)}, u32[]{:S(2)}) %collective-permute-start) | collective-permute-done | bytes 131104 | tf_op jit(solution)/shard_map/ppermute | solution.py:347
  3.9 2.9 %collective-permute-start.1 = (f32[2,128,128]{2,1,0:T(8,128)S(1)}, f32[2,128,128]{2,1,0:T(8,128)S(1)}, u32[]{:S(2)}, u32[]{:S(2)}) collective-permute-start(f32[2,128,128]{2,1,0:T(8,128)S(1)} %broadcast_select_fusion), channel_id=1, source_target_pairs={{0,2},{1,3},{2,0},{3,1},{4,6},{5,7},{6,4},{7,5},{8,10},{9,11},{10,... | collective-permute-start | bytes 393224 | tf_op jit(solution)/shard_map/ppermute | solution.py:347
  6.9 1.3 %collective-permute-start.3 = (f32[2,128,384]{2,1,0:T(8,128)S(1)}, f32[2,128,384]{2,1,0:T(8,128)S(1)}, u32[]{:S(2)}, u32[]{:S(2)}) collective-permute-start(f32[2,128,384]{2,1,0:T(8,128)S(1)} %get-tuple-element.45), channel_id=1, source_target_pairs={{1,0},{2,1},{3,2},{4,3},{5,4},{6,5},{7,6},{8,7},{9,8},{10,9},{11,1... | collective-permute-start | bytes 1179656 | tf_op jit(solution)/shard_map/ppermute | solution.py:364
  8.2 2.5 %collective-permute-done.1 = f32[2,128,128]{2,1,0:T(8,128)S(1)} collective-permute-done((f32[2,128,128]{2,1,0:T(8,128)S(1)}, f32[2,128,128]{2,1,0:T(8,128)S(1)}, u32[]{:S(2)}, u32[]{:S(2)}) %collective-permute-start.1) | collective-permute-done | bytes 131104 | tf_op jit(solution)/shard_map/ppermute | solution.py:347
  10.7 1.9 %collective-permute-start.2 = (f32[2,128,128]{2,1,0:T(8,128)S(1)}, f32[2,128,128]{2,1,0:T(8,128)S(1)}, u32[]{:S(2)}, u32[]{:S(2)}) collective-permute-start(f32[2,128,128]{2,1,0:T(8,128)S(1)} %broadcast_select_fusion.1), channel_id=1, source_target_pairs={{0,4},{1,5},{2,6},{3,7},{4,0},{5,1},{6,2},{7,3},{8,12},{9,13},{10,... | collective-permute-start | bytes 393224 | tf_op jit(solution)/shard_map/ppermute | solution.py:347
  12.6 1.8 %shard_map.141 = (f32[2,384,384]{2,1,0:T(8,128)S(1)}, bf16[128,512]{1,0:T(8,128)(2,1)S(1)}, bf16[512,128]{1,0:T(8,128)(2,1)S(1)}, bf16[2,768,256]{2,1,0:T(8,128)(2,1)S(1)}, bf16[2,256,768]{2,1,0:T(8,128)(2,1)S(1)}) custom-call(f32[2,384,384]{2,1,0:T(8,128)} %refs_0_, bf16[128,512]{1,0:T(8,128)(2,1)} %constant.24.clone.refs_1_, ...), custom_call_target="tpu_custom_call" | custom-call | bytes 6029312 | tf_op jit(solution)/shard_map/pallas_call | solution.py:256
  14.4 4.5 %collective-permute-done.2 = f32[2,128,128]{2,1,0:T(8,128)S(1)} collective-permute-done((f32[2,128,128]{2,1,0:T(8,128)S(1)}, f32[2,128,128]{2,1,0:T(8,128)S(1)}, u32[]{:S(2)}, u32[]{:S(2)}) %collective-permute-start.2) | collective-permute-done | bytes 131104 | tf_op jit(solution)/shard_map/ppermute | solution.py:347
  18.9 0.0 collective-permute-done.3.halo
  18.9 2.9 %collective-permute-start.4 = (f32[2,128,128]{2,1,0:T(8,128)S(1)}, f32[2,128,128]{2,1,0:T(8,128)S(1)}, u32[]{:S(2)}, u32[]{:S(2)}) collective-permute-start(f32[2,128,128]{2,1,0:T(8,128)S(1)} %broadcast_select_fusion.2), channel_id=1, source_target_pairs={{0,8},{1,9},{2,10},{3,11},{4,12},{5,13},{6,14},{7,15},{8,0},{9,1},... | collective-permute-start | bytes 393224 | tf_op jit(solution)/shard_map/ppermute | solution.py:347
  21.8 0.0 copy-start
  21.8 0.0 copy-start.1
  21.8 0.0 copy-start.2
  21.8 0.0 copy-start.3
  21.8 3.2 %shard_map.142 = (f32[2,4,256,256]{3,2,1,0:T(8,128)S(1)}, f32[384,384]{1,0:T(8,128)S(1)}) custom-call(f32[2,384,384]{2,1,0:T(8,128)S(1)} %get-tuple-element.52.tile, f32[2,128,384]{2,1,0:T(8,128)S(1)} %collective-permute-done.3.halo, bf16[128,512]{1,0:T(8,128)(2,1)S(1)} %get-tuple-element.54.band_rows, bf16[512,128]{1,0:T(8,128)(2,1)S(1)} %get-tuple-element.55.band_cols, ...), custom_call_target="tpu_custom_call" | custom-call | flops 2000000000 | bytes 6000000 | tf_op jit(solution)/shard_map/pallas_call | solution.py:272
  25.0 0.2 collective-permute-done.4
  25.3 0.1 collective-permute-start.5
  25.4 1.5 %collective-permute-start.6 = (f32[2,128,128]{2,1,0:T(8,128)S(1)}, f32[2,128,128]{2,1,0:T(8,128)S(1)}, u32[]{:S(2)}, u32[]{:S(2)}) collective-permute-start(f32[2,128,128]{2,1,0:T(8,128)S(1)} %broadcast_select_fusion.3.refs_0_), channel_id=1, source_target_pairs={{0,16},{16,0},{1,17},{17,1},{2,18},{18,2},{3,19},{19,3},{4,20},{20... | collective-permute-start | bytes 393224 | tf_op jit(solution)/shard_map/ppermute | solution.py:347
  26.9 0.0 collective-permute-done.5.refs_1_
  26.9 0.0 copy-done
  26.9 0.0 copy-done.1
  26.9 0.0 copy-done.2
  26.9 0.0 copy-done.3
  26.9 4.1 %shard_map.143 = (f32[2,384,384]{2,1,0:T(8,128)S(1)}, f32[2,2]{1,0:T(2,128)S(1)}) custom-call(f32[2,128,128]{2,1,0:T(8,128)S(1)} %broadcast_select_fusion.3.refs_0_, f32[2,128,128]{2,1,0:T(8,128)S(1)} %collective-permute-done.5.refs_1_, s32[8,128]{1,0:T(8,128)S(1)} %get-tuple-element.61.refs_2_.refs_1_, ...), custom_call_target="tpu_custom_call" | custom-call | flops 2600000000 | bytes 6000000 | tf_op jit(solution)/shard_map/pallas_call | solution.py:302
  31.1 0.2 collective-permute-done.6.refs_0_
  31.3 0.1 collective-permute-start.7
  31.3 2.3 %shard_map.144 = (f32[1,384,384]{2,1,0:T(8,128)S(1)}, f32[2,2]{1,0:T(2,128)S(1)}) custom-call(f32[2,128,128]{2,1,0:T(8,128)S(1)} %collective-permute-done.6.refs_0_, s32[8,128]{1,0:T(8,128)S(1)} %get-tuple-element.61.refs_2_.refs_1_, f32[2,4,256,256]{3,2,1,0:T(8,128)S(1)} %get-tuple-element.62.refs_3_.refs_2_, ...), custom_call_target="tpu_custom_call" | custom-call | flops 1300000000 | bytes 6000000 | tf_op jit(solution)/shard_map/pallas_call | solution.py:302
  33.6 0.0 collective-permute-done.7.refs_0_
  33.6 2.3 %shard_map.145 = (f32[1,384,384]{2,1,0:T(8,128)S(1)}, f32[2,2]{1,0:T(2,128)S(1)}) custom-call(f32[2,128,128]{2,1,0:T(8,128)S(1)} %collective-permute-done.7.refs_0_, s32[8,128]{1,0:T(8,128)S(1)} %get-tuple-element.61.refs_2_.refs_1_, f32[2,4,256,256]{3,2,1,0:T(8,128)S(1)} %get-tuple-element.62.refs_3_.refs_2_, ...), custom_call_target="tpu_custom_call" | custom-call | flops 1300000000 | bytes 6000000 | tf_op jit(solution)/shard_map/pallas_call | solution.py:302
  36.0 2.4 %collective-permute-start.8 = (f32[2,2]{1,0:T(2,128)S(1)}, f32[2,2]{1,0:T(2,128)S(1)}, u32[]{:S(2)}, u32[]{:S(2)}) collective-permute-start(f32[2,2]{1,0:T(2,128)S(1)} %maximum_maximum_fusion), channel_id=1, source_target_pairs={{0,2},{1,3},{2,0},{3,1},{4,6},{5,7},{6,4},{7,5},{8,10},{9,11},{10,... | collective-permute-start | bytes 56 | tf_op jit(solution)/shard_map/ppermute | solution.py:347
  38.3 1.5 %collective-permute-done.8 = f32[2,2]{1,0:T(2,128)S(1)} collective-permute-done((f32[2,2]{1,0:T(2,128)S(1)}, f32[2,2]{1,0:T(2,128)S(1)}, u32[]{:S(2)}, u32[]{:S(2)}) %collective-permute-start.8) | collective-permute-done | bytes 48 | tf_op jit(solution)/shard_map/ppermute | solution.py:347
  39.9 0.0 collective-permute-start.9
  39.9 1.4 %shard_map.146 = f32[4,384,384]{2,1,0:T(8,128)} custom-call(f32[2,384,384]{2,1,0:T(8,128)S(1)} %get-tuple-element.75.refs_0_, f32[1,384,384]{2,1,0:T(8,128)S(1)} %get-tuple-element.76.refs_1_, f32[1,384,384]{2,1,0:T(8,128)S(1)} %get-tuple-element.77.refs_2_), custom_call_target="tpu_custom_call" | custom-call | bytes 4718592 | tf_op jit(solution)/shard_map/pallas_call | solution.py:333
  41.3 2.1 %collective-permute-done.9 = f32[2,2]{1,0:T(2,128)S(1)} collective-permute-done((f32[2,2]{1,0:T(2,128)S(1)}, f32[2,2]{1,0:T(2,128)S(1)}, u32[]{:S(2)}, u32[]{:S(2)}) %collective-permute-start.9) | collective-permute-done | bytes 48 | tf_op jit(solution)/shard_map/ppermute | solution.py:347
  43.5 2.1 %collective-permute-start.10 = (f32[2,2]{1,0:T(2,128)S(1)}, f32[2,2]{1,0:T(2,128)S(1)}, u32[]{:S(2)}, u32[]{:S(2)}) collective-permute-start(f32[2,2]{1,0:T(2,128)S(1)} %max.21), channel_id=1, source_target_pairs={{0,8},{1,9},{2,10},{3,11},{4,12},{5,13},{6,14},{7,15},{8,0},{9,1},... | collective-permute-start | bytes 56 | tf_op jit(solution)/shard_map/ppermute | solution.py:347
  45.6 2.3 %collective-permute-done.10 = f32[2,2]{1,0:T(2,128)S(1)} collective-permute-done((f32[2,2]{1,0:T(2,128)S(1)}, f32[2,2]{1,0:T(2,128)S(1)}, u32[]{:S(2)}, u32[]{:S(2)}) %collective-permute-start.10) | collective-permute-done | bytes 48 | tf_op jit(solution)/shard_map/ppermute | solution.py:347
  47.9 0.0 collective-permute-start.11
  47.9 1.1 %collective-permute-done.11 = f32[2,2]{1,0:T(2,128)S(1)} collective-permute-done((f32[2,2]{1,0:T(2,128)S(1)}, f32[2,2]{1,0:T(2,128)S(1)}, u32[]{:S(2)}, u32[]{:S(2)}) %collective-permute-start.11) | collective-permute-done | bytes 48 | tf_op jit(solution)/shard_map/ppermute | solution.py:347
  49.1 0.6 %max.23 = f32[2,2]{1,0:T(2,128)} maximum(f32[2,2]{1,0:T(2,128)S(1)} %max.22, f32[2,2]{1,0:T(2,128)S(1)} %collective-permute-done.11) | non-fusion elementwise | flops 4 | bytes 48 | tf_op jit(solution)/shard_map/max | solution.py:401
  (9 shorter events, 0.1 us)
Async XLA Ops:
  2.4 1.5 %collective-permute-start = (f32[2,128,128]{2,1,0:T(8,128)S(1)}, f32[2,128,128]{2,1,0:T(8,128)S(1)}, u32[]{:S(2)}, u32[]{:S(2)}) collective-permute-start(f32[2,128,128]{2,1,0:T(8,128)S(1)} %get-tuple-element.43), channel_id=1, source_target_pairs={{0,1},{1,0},{2,3},{3,2},{4,5},{5,4},{6,7},{7,6},{8,9},{9,8},{10,11... | collective-permute-start | bytes 393224 | tf_op jit(solution)/shard_map/ppermute | solution.py:347
  3.9 6.8 %collective-permute-start.1 = (f32[2,128,128]{2,1,0:T(8,128)S(1)}, f32[2,128,128]{2,1,0:T(8,128)S(1)}, u32[]{:S(2)}, u32[]{:S(2)}) collective-permute-start(f32[2,128,128]{2,1,0:T(8,128)S(1)} %broadcast_select_fusion), channel_id=1, source_target_pairs={{0,2},{1,3},{2,0},{3,1},{4,6},{5,7},{6,4},{7,5},{8,10},{9,11},{10,... | collective-permute-start | bytes 393224 | tf_op jit(solution)/shard_map/ppermute | solution.py:347
  6.9 12.0 %collective-permute-start.3 = (f32[2,128,384]{2,1,0:T(8,128)S(1)}, f32[2,128,384]{2,1,0:T(8,128)S(1)}, u32[]{:S(2)}, u32[]{:S(2)}) collective-permute-start(f32[2,128,384]{2,1,0:T(8,128)S(1)} %get-tuple-element.45), channel_id=1, source_target_pairs={{1,0},{2,1},{3,2},{4,3},{5,4},{6,5},{7,6},{8,7},{9,8},{10,9},{11,1... | collective-permute-start | bytes 1179656 | tf_op jit(solution)/shard_map/ppermute | solution.py:364
  10.7 8.2 %collective-permute-start.2 = (f32[2,128,128]{2,1,0:T(8,128)S(1)}, f32[2,128,128]{2,1,0:T(8,128)S(1)}, u32[]{:S(2)}, u32[]{:S(2)}) collective-permute-start(f32[2,128,128]{2,1,0:T(8,128)S(1)} %broadcast_select_fusion.1), channel_id=1, source_target_pairs={{0,4},{1,5},{2,6},{3,7},{4,0},{5,1},{6,2},{7,3},{8,12},{9,13},{10,... | collective-permute-start | bytes 393224 | tf_op jit(solution)/shard_map/ppermute | solution.py:347
  18.9 6.3 %collective-permute-start.4 = (f32[2,128,128]{2,1,0:T(8,128)S(1)}, f32[2,128,128]{2,1,0:T(8,128)S(1)}, u32[]{:S(2)}, u32[]{:S(2)}) collective-permute-start(f32[2,128,128]{2,1,0:T(8,128)S(1)} %broadcast_select_fusion.2), channel_id=1, source_target_pairs={{0,8},{1,9},{2,10},{3,11},{4,12},{5,13},{6,14},{7,15},{8,0},{9,1},... | collective-permute-start | bytes 393224 | tf_op jit(solution)/shard_map/ppermute | solution.py:347
  21.8 5.1 %copy-start = (bf16[2,768,256]{2,1,0:T(8,128)(2,1)S(1)}, bf16[2,768,256]{2,1,0:T(8,128)(2,1)}, u32[]{:S(2)}) copy-start(bf16[2,768,256]{2,1,0:T(8,128)(2,1)} %constant.23.clone.refs_8_.refs_7_) | copy-start | bytes 2359300
  21.8 5.1 %copy-start.1 = (bf16[2,256,768]{2,1,0:T(8,128)(2,1)S(1)}, bf16[2,256,768]{2,1,0:T(8,128)(2,1)}, u32[]{:S(2)}) copy-start(bf16[2,256,768]{2,1,0:T(8,128)(2,1)} %constant.22.clone.refs_7_.refs_6_) | copy-start | bytes 2359300
  21.8 5.1 %copy-start.2 = (bf16[384,512]{1,0:T(8,128)(2,1)S(1)}, bf16[384,512]{1,0:T(8,128)(2,1)}, u32[]{:S(2)}) copy-start(bf16[384,512]{1,0:T(8,128)(2,1)} %constant.21.clone.refs_6_.refs_5_) | copy-start | bytes 1179652
  21.8 5.1 %copy-start.3 = (bf16[512,384]{1,0:T(8,128)(2,1)S(1)}, bf16[512,384]{1,0:T(8,128)(2,1)}, u32[]{:S(2)}) copy-start(bf16[512,384]{1,0:T(8,128)(2,1)} %constant.20.clone.refs_5_.refs_4_) | copy-start | bytes 1179652
  25.3 1.6 %collective-permute-start.5 = (f32[2,128,128]{2,1,0:T(8,128)S(1)}, f32[2,128,128]{2,1,0:T(8,128)S(1)}, u32[]{:S(2)}, u32[]{:S(2)}) collective-permute-start(f32[2,128,128]{2,1,0:T(8,128)S(1)} %broadcast_select_fusion.3.refs_0_), channel_id=1, source_target_pairs={{0,1},{1,0},{2,3},{3,2},{4,5},{5,4},{6,7},{7,6},{8,9},{9,8},{10,11... | collective-permute-start | bytes 393224 | tf_op jit(solution)/shard_map/ppermute | solution.py:347
  25.4 5.9 %collective-permute-start.6 = (f32[2,128,128]{2,1,0:T(8,128)S(1)}, f32[2,128,128]{2,1,0:T(8,128)S(1)}, u32[]{:S(2)}, u32[]{:S(2)}) collective-permute-start(f32[2,128,128]{2,1,0:T(8,128)S(1)} %broadcast_select_fusion.3.refs_0_), channel_id=1, source_target_pairs={{0,16},{16,0},{1,17},{17,1},{2,18},{18,2},{3,19},{19,3},{4,20},{20... | collective-permute-start | bytes 393224 | tf_op jit(solution)/shard_map/ppermute | solution.py:347
  31.3 2.4 %collective-permute-start.7 = (f32[2,128,128]{2,1,0:T(8,128)S(1)}, f32[2,128,128]{2,1,0:T(8,128)S(1)}, u32[]{:S(2)}, u32[]{:S(2)}) collective-permute-start(f32[2,128,128]{2,1,0:T(8,128)S(1)} %collective-permute-done.6.refs_0_), channel_id=1, source_target_pairs={{0,1},{1,0},{2,3},{3,2},{4,5},{5,4},{6,7},{7,6},{8,9},{9,8},{10,11... | collective-permute-start | bytes 393224 | tf_op jit(solution)/shard_map/ppermute | solution.py:347
  36.0 3.9 %collective-permute-start.8 = (f32[2,2]{1,0:T(2,128)S(1)}, f32[2,2]{1,0:T(2,128)S(1)}, u32[]{:S(2)}, u32[]{:S(2)}) collective-permute-start(f32[2,2]{1,0:T(2,128)S(1)} %maximum_maximum_fusion), channel_id=1, source_target_pairs={{0,2},{1,3},{2,0},{3,1},{4,6},{5,7},{6,4},{7,5},{8,10},{9,11},{10,... | collective-permute-start | bytes 56 | tf_op jit(solution)/shard_map/ppermute | solution.py:347
  39.9 3.6 %collective-permute-start.9 = (f32[2,2]{1,0:T(2,128)S(1)}, f32[2,2]{1,0:T(2,128)S(1)}, u32[]{:S(2)}, u32[]{:S(2)}) collective-permute-start(f32[2,2]{1,0:T(2,128)S(1)} %max.20), channel_id=1, source_target_pairs={{0,4},{1,5},{2,6},{3,7},{4,0},{5,1},{6,2},{7,3},{8,12},{9,13},{10,... | collective-permute-start | bytes 56 | tf_op jit(solution)/shard_map/ppermute | solution.py:347
  43.5 4.5 %collective-permute-start.10 = (f32[2,2]{1,0:T(2,128)S(1)}, f32[2,2]{1,0:T(2,128)S(1)}, u32[]{:S(2)}, u32[]{:S(2)}) collective-permute-start(f32[2,2]{1,0:T(2,128)S(1)} %max.21), channel_id=1, source_target_pairs={{0,8},{1,9},{2,10},{3,11},{4,12},{5,13},{6,14},{7,15},{8,0},{9,1},... | collective-permute-start | bytes 56 | tf_op jit(solution)/shard_map/ppermute | solution.py:347
  47.9 1.1 %collective-permute-start.11 = (f32[2,2]{1,0:T(2,128)S(1)}, f32[2,2]{1,0:T(2,128)S(1)}, u32[]{:S(2)}, u32[]{:S(2)}) collective-permute-start(f32[2,2]{1,0:T(2,128)S(1)} %max.22), channel_id=1, source_target_pairs={{0,1},{1,0},{2,3},{3,2},{4,5},{5,4},{6,7},{7,6},{8,9},{9,8},{10,11... | collective-permute-start | bytes 56 | tf_op jit(solution)/shard_map/ppermute | solution.py:347
